TPU v7x, 128 devices: a whole 4x4x4 slice. The times are simulated.
128 devices in a mesh: group: 8 (over x, core), local: 16 (over z, y).
Axes of the slice: x: 4, y: 4, z: 4, core: 2. Of those that a mesh axis runs over, the one named last changes fastest.
Arguments:
- tokens: bfloat16 [1024, 7168], P(('group', 'local')), may hold values from -6 to 6
- picked_group_index: int32 [1024, 4], P(('group', 'local')), may hold values from 0 to 7, as said below
- picked_expert_index: int32 [1024, 8], P(('group', 'local')), may hold values from 0 to 23, as said below
- routing_pick_weight: bfloat16 [1024, 8], P(('group', 'local')), may hold values from 0.099609375 to 0.59765625
- common_gate_weight: bfloat16 [7168, 2048], P(None, 'local'), may hold values from -0.0625 to 0.0625
- common_up_weight: bfloat16 [7168, 2048], P(None, 'local'), may hold values from -0.0625 to 0.0625
- common_down_weight: bfloat16 [2048, 7168], P('local'), may hold values from -0.125 to 0.125
- routed_gate_weight: bfloat16 [24, 7168, 2048], P('group', None, 'local'), may hold values from -0.0625 to 0.0625
- routed_up_weight: bfloat16 [24, 7168, 2048], P('group', None, 'local'), may hold values from -0.0625 to 0.0625
- routed_down_weight: bfloat16 [24, 2048, 7168], P('group', 'local'), may hold values from -0.125 to 0.125
- gate_block_scales: float32 [24, 56, 16], P('group', None, 'local'), may hold values from 0.5 to 2
- up_block_scales: float32 [24, 56, 16], P('group', None, 'local'), may hold values from 0.5 to 2
- down_block_scales: float32 [24, 16, 56], P('group', 'local'), may hold values from 0.5 to 2
- adapter_input_maps: bfloat16 [24, 7168, 32], P('group'), may hold values from -0.0625 to 0.0625
- adapter_output_maps: bfloat16 [24, 2, 16, 2048], P('group', None, None, 'local'), may hold values from -1.5 to 1.5
- adapter_down_input: bfloat16 [24, 2048, 16], P('group', 'local'), may hold values from -0.125 to 0.125
- adapter_down_output: bfloat16 [24, 16, 7168], P('group'), may hold values from -1.5 to 1.5
Outputs:
- mixed: bfloat16 [1024, 7168], P(('group', 'local'))
Inputs may be any that keep to these rules, and one draw needn't show every extreme that they name: `picked_group_index`: each row names 4 different groups. Among the rows of one device every group is named by exactly 4 rows. `picked_expert_index`: each row names 8 different experts, each in a group that the same row of picked_group_index names.
All inputs are finite; a program needn't handle non-finite values.
Results may differ from a plain program's by a relative error of at most 0.02.
Values may be sent and summed in bfloat16 or wider, within the bound.
A program may use at most 128 MiB of HBM per device.

v0:
```python
import jax
import jax.numpy as jnp
from jax import lax
from jax.sharding import PartitionSpec as P

TOPK_GROUP = 4
QB = 128


def dequant(weight, scale):
    expanded = jnp.repeat(jnp.repeat(scale, QB, axis=1), QB, axis=2)
    return (weight.astype(jnp.float32) * expanded).astype(jnp.bfloat16)


def on_device(
    tokens,
    picked_group_index,
    picked_expert_index,
    routing_pick_weight,
    common_gate_weight,
    common_up_weight,
    common_down_weight,
    routed_gate_weight,
    routed_up_weight,
    routed_down_weight,
    gate_block_scales,
    up_block_scales,
    down_block_scales,
    adapter_input_maps,
    adapter_output_maps,
    adapter_down_input,
    adapter_down_output,
):
    group_count = lax.axis_size("group")
    local_count = lax.axis_size("local")
    token_count = tokens.shape[0]
    width_of_model = tokens.shape[1]
    experts_per_group = routed_gate_weight.shape[0]
    slice_hidden_count = routed_gate_weight.shape[2]
    adapter_rank_rows = adapter_down_output.shape[1]
    capacity = min(token_count, token_count * TOPK_GROUP // group_count + token_count // 16)
    shard_rows = lax.all_gather(tokens, "local", axis=0, tiled=True)
    gate_activation = jnp.dot(shard_rows, common_gate_weight, preferred_element_type=jnp.float32)
    up_activation = jnp.dot(shard_rows, common_up_weight, preferred_element_type=jnp.float32)
    shared_hid = (jax.nn.silu(gate_activation) * up_activation).astype(jnp.bfloat16)
    shared_out = lax.psum_scatter(
        jnp.dot(shared_hid, common_down_weight, preferred_element_type=jnp.float32).astype(
            jnp.bfloat16
        ),
        "local",
        scatter_dimension=0,
        tiled=True,
    ).astype(jnp.float32)
    gate_cat = (
        dequant(routed_gate_weight, gate_block_scales)
        .transpose(1, 0, 2)
        .reshape(width_of_model, experts_per_group * slice_hidden_count)
    )
    up_cat = (
        dequant(routed_up_weight, up_block_scales)
        .transpose(1, 0, 2)
        .reshape(width_of_model, experts_per_group * slice_hidden_count)
    )
    down_cat = dequant(routed_down_weight, down_block_scales).reshape(
        experts_per_group * slice_hidden_count, width_of_model
    )
    adapter_input_rows = adapter_input_maps.transpose(1, 0, 2).reshape(
        width_of_model, experts_per_group * 2 * adapter_rank_rows
    )
    group_numbers = jnp.arange(group_count, dtype=jnp.int32)
    member = jnp.any(picked_group_index[:, :, None] == group_numbers[None, None, :], axis=1).astype(
        jnp.int32
    )
    slot_index = jnp.cumsum(member, axis=0) - member
    slot_numbers = jnp.arange(capacity, dtype=jnp.int32)
    placed = (slot_index.T[:, None, :] == slot_numbers[None, :, None]) & (member.T[:, None, :] == 1)
    dispatch = placed.astype(jnp.bfloat16)
    expert_numbers = jnp.arange(group_count * experts_per_group, dtype=jnp.int32)
    pick_weight = jnp.sum(
        jnp.where(
            picked_expert_index[:, :, None] == expert_numbers[None, None, :],
            routing_pick_weight.astype(jnp.float32)[:, :, None],
            0.0,
        ),
        axis=1,
    )
    pick_weight = pick_weight.reshape(token_count, group_count, experts_per_group)
    rows_out = jnp.einsum(
        "gst,td->gsd", dispatch, tokens, preferred_element_type=jnp.float32
    ).astype(jnp.bfloat16)
    weights_out = jnp.einsum("gst,tgj->gsj", placed.astype(jnp.float32), pick_weight).astype(
        jnp.bfloat16
    )
    send_rows = jnp.broadcast_to(
        rows_out[:, None], (group_count, local_count, capacity, width_of_model)
    ).reshape(-1, width_of_model)
    send_weights = jnp.broadcast_to(
        weights_out[:, None], (group_count, local_count, capacity, experts_per_group)
    ).reshape(-1, experts_per_group)
    arrived_rows, arrived_weights = (
        lax.all_to_all(send_rows, ("group", "local"), split_axis=0, concat_axis=0, tiled=True),
        lax.all_to_all(send_weights, ("group", "local"), split_axis=0, concat_axis=0, tiled=True),
    )
    row_count = arrived_rows.shape[0]
    adapter_hidden_rows = (
        jnp.dot(arrived_rows, adapter_input_rows, preferred_element_type=jnp.float32)
        .astype(jnp.bfloat16)
        .reshape(row_count, experts_per_group, 2, adapter_rank_rows)
    )
    gate_activation = jnp.dot(arrived_rows, gate_cat, preferred_element_type=jnp.float32).reshape(
        row_count, experts_per_group, slice_hidden_count
    )
    gate_activation = gate_activation + jnp.einsum(
        "abt,btw->abw",
        adapter_hidden_rows[:, :, 0],
        adapter_output_maps[:, 0],
        preferred_element_type=jnp.float32,
    )
    up_activation = jnp.dot(arrived_rows, up_cat, preferred_element_type=jnp.float32).reshape(
        row_count, experts_per_group, slice_hidden_count
    )
    up_activation = up_activation + jnp.einsum(
        "abt,btw->abw",
        adapter_hidden_rows[:, :, 1],
        adapter_output_maps[:, 1],
        preferred_element_type=jnp.float32,
    )
    activated = (
        jax.nn.silu(gate_activation)
        * up_activation
        * arrived_weights.astype(jnp.float32)[:, :, None]
    )
    hidden_units = activated.astype(jnp.bfloat16).reshape(
        row_count, experts_per_group * slice_hidden_count
    )
    project_row_count = hidden_units.shape[0]
    adapter_down_term = jnp.einsum(
        "ref,efk->rek",
        hidden_units.reshape(project_row_count, experts_per_group, slice_hidden_count),
        adapter_down_input,
        preferred_element_type=jnp.float32,
    ).astype(jnp.bfloat16)
    base_part = jnp.dot(hidden_units, down_cat, preferred_element_type=jnp.float32)
    partials = (
        base_part
        + jnp.einsum(
            "zgt,gtb->zb",
            adapter_down_term,
            adapter_down_output,
            preferred_element_type=jnp.float32,
        )
    ).astype(jnp.bfloat16)
    returned = lax.all_to_all(
        partials, ("group", "local"), split_axis=0, concat_axis=0, tiled=True
    ).reshape(group_count, local_count, capacity, width_of_model)
    group_out = jnp.sum(returned, axis=1, dtype=jnp.float32).astype(jnp.bfloat16)
    routed = jnp.einsum("gst,gsd->td", dispatch, group_out, preferred_element_type=jnp.float32)
    return (shared_out + routed).astype(jnp.bfloat16)


def solution(mesh):
    in_specs = (
        P(("group", "local"), None),
        P(("group", "local"), None),
        P(("group", "local"), None),
        P(("group", "local"), None),
        P(None, "local"),
        P(None, "local"),
        P("local", None),
        P("group", None, "local"),
        P("group", None, "local"),
        P("group", "local", None),
        P("group", None, "local"),
        P("group", None, "local"),
        P("group", "local", None),
        P("group", None, None),
        P("group", None, None, "local"),
        P("group", "local", None),
        P("group", None, None),
    )
    out_specs = P(("group", "local"), None)
    return jax.shard_map(
        on_device, mesh=mesh, in_specs=in_specs, out_specs=out_specs, check_vma=False
    )
```

profile of v0, /device:TPU:1, one launch (start us, length us, event | category | flops | bytes accessed | tf_op | source)
XLA Modules:
  0.0 427.0 jit_solution(9284920426993396399)
XLA Ops:
  6.5 0.0 copy-start
  6.5 0.9 fusion.28
  7.5 0.1 copy.71
  7.6 0.7 convert_element_type.84
  8.3 0.8 select_reduce_fusion
  9.1 0.1 copy.70
  9.2 0.1 fusion.36
  9.3 0.7 broadcast_in_dim.60
  10.0 11.5 %all-to-all-start.1 = ((bf16[128,4,3]{1,2,0:T(4,128)(2,1)}), bf16[128,4,3]{1,2,0:T(4,128)(2,1)S(1)}, u32[]{:S(2)}, u32[]{:S(2)}) async-start(bf16[128,4,3]{1,2,0:T(4,128)(2,1)} %bitcast.21), calls=%async_computation.1 | async-start | bytes 262144 | tf_op jit(solution)/shard_map/all_to_all | solution.py:102
  21.5 0.0 copy-done.5
  21.5 1.2 convolution_convert_fusion.1
  22.7 0.4 copy.63
  23.1 8.6 %all-to-all-done.1 = bf16[128,4,3]{1,2,0:T(4,128)(2,1)S(1)} async-done(((bf16[128,4,3]{1,2,0:T(4,128)(2,1)}), bf16[128,4,3]{1,2,0:T(4,128)(2,1)S(1)}, u32[]{:S(2)}, u32[]{:S(2)}) %all-to-all-start.1) | async-done | bytes 3104 | tf_op jit(solution)/shard_map/all_to_all | solution.py:102
  31.7 5.3 %broadcast_in_dim.30 = bf16[8,16,4,7168]{3,2,1,0:T(4,128)(2,1)} broadcast(bf16[8,4,7168]{2,1,0:T(4,128)(2,1)S(1)} %copy.63), dimensions={0,2,3} | broadcast | bytes 7798784 | tf_op jit(solution)/shard_map/broadcast_in_dim | solution.py:94
  37.0 5.0 %all-to-all-start = ((bf16[128,4,7168]{2,1,0:T(4,128)(2,1)}), bf16[128,4,7168]{2,1,0:T(4,128)(2,1)}, u32[]{:S(2)}, u32[]{:S(2)}) async-start(bf16[128,4,7168]{2,1,0:T(4,128)(2,1)} %bitcast.129), calls=%async_computation | async-start | bytes 14680064 | tf_op jit(solution)/shard_map/all_to_all | solution.py:101
  42.0 0.0 copy-start.10
  42.0 8.3 %copy.67 = bf16[3,7168,128]{1,2,0:T(8,128)(2,1)} copy(bf16[3,7168,128]{2,1,0:T(8,128)(2,1)} %param.25) | data formatting | bytes 11010048 | tf_op args[8]
  50.3 0.0 copy-done.10
  50.3 0.1 broadcast_bitcast_fusion.1
  50.4 0.0 copy-start.11
  50.4 0.0 copy-start.12
  50.4 8.3 %copy.64 = bf16[3,7168,128]{1,2,0:T(8,128)(2,1)} copy(bf16[3,7168,128]{2,1,0:T(8,128)(2,1)} %param.24) | data formatting | bytes 11010048 | tf_op args[7]
  58.7 0.0 copy-done.11
  58.7 0.1 broadcast_bitcast_fusion.2
  58.9 0.0 copy-done.12
  58.9 0.1 broadcast_bitcast_fusion
  59.0 0.1 copy.72
  59.1 0.2 copy.73
  59.3 0.8 reshape.78
  60.0 71.3 %all-to-all-done = bf16[128,4,7168]{2,1,0:T(4,128)(2,1)} async-done(((bf16[128,4,7168]{2,1,0:T(4,128)(2,1)}), bf16[128,4,7168]{2,1,0:T(4,128)(2,1)}, u32[]{:S(2)}, u32[]{:S(2)}) %all-to-all-start) | async-done | bytes 7340064 | tf_op jit(solution)/shard_map/all_to_all | solution.py:101
  131.4 12.2 %reshape.80 = bf16[512,7168,1]{1,0,2:T(8,128)(2,1)} reshape(bf16[128,4,7168]{2,1,0:T(4,128)(2,1)} %all-to-all-done) | data formatting | bytes 14680064 | tf_op jit(solution)/shard_map/all_to_all | solution.py:101
  143.6 8.7 %fusion.7 = f32[512,3,128]{2,0,1:T(8,128)} fusion(bf16[512,7168,1]{1,0,2:T(8,128)(2,1)} %reshape.80, bf16[3,7168,128]{1,2,0:T(8,128)(2,1)} %copy.67, f32[3,7168]{1,0:T(4,128)S(1)} %bitcast.138), kind=kOutput, calls=%fused_computation.14 | convolution fusion | flops 2826829824 | bytes 13717504 | tf_op jit(solution)/shard_map/dot_general | solution.py:119
  152.4 0.0 slice-done.2
  152.4 0.0 copy-done.1
  152.4 5.1 %fusion.4 = f32[512,3,128]{2,0,1:T(8,128)} fusion(bf16[512,7168,1]{1,0,2:T(8,128)(2,1)S(1)} %copy-done.1, bf16[3,7168,128]{1,2,0:T(8,128)(2,1)S(1)} %bitcast.133, f32[3,7168]{1,0:T(4,128)S(1)} %bitcast.139), kind=kOutput, calls=%fused_computation.12 | convolution fusion | flops 2826829824 | bytes 13717504 | tf_op jit(solution)/shard_map/dot_general | solution.py:110
  157.5 12.2 %all_to_all.22 = bf16[512,7168]{1,0:T(8,128)(2,1)} reshape(bf16[128,4,7168]{2,1,0:T(4,128)(2,1)} %all-to-all-done) | data formatting | bytes 14680064 | tf_op jit(solution)/shard_map/all_to_all | solution.py:101
  169.7 0.0 slice-start
  169.8 0.0 slice-start.1
  169.8 5.6 %convolution_convert_fusion.2 = bf16[512,96]{0,1:T(8,128)(2,1)S(1)} fusion(bf16[512,7168]{1,0:T(8,128)(2,1)} %all_to_all.22, bf16[7168,96]{0,1:T(8,128)(2,1)S(1)} %bitcast.134), kind=kOutput, calls=%fused_computation.26 | convolution fusion | flops 704692224 | bytes 8814592 | tf_op jit(solution)/shard_map/dot_general | solution.py:106
  175.4 0.3 fusion.16
  175.7 0.0 copy-done.8
  175.7 0.0 copy-done.14
  175.8 0.5 fusion.17
  176.3 0.0 copy-start.4
  176.3 0.0 copy-start.7
  176.3 7.2 %fusion.9 = f32[512,7168,1]{1,0,2:T(8,128)} fusion(bf16[512,3,128]{2,0,1:T(8,128)(2,1)S(1)} %fusion.17, bf16[3,128,7168]{2,1,0:T(8,128)(2,1)S(1)} %bitcast.131, f32[3,7168]{1,0:T(4,128)S(1)} %bitcast.135), kind=kOutput, calls=%fused_computation.15 | convolution fusion | flops 2826829824 | bytes 20664320 | tf_op jit(solution)/shard_map/dot_general | solution.py:143
  183.5 0.0 copy-done.4
  183.5 8.6 %fusion = bf16[512,7168]{1,0:T(8,128)(2,1)} fusion(f32[512,7168,1]{1,0,2:T(8,128)} %fusion.9, bf16[3,16,7168]{2,1,0:T(8,128)(2,1)S(1)} %copy-done.4, bf16[512,3,128]{2,0,1:T(8,128)(2,1)S(1)} %fusion.17, bf16[3,128,16]{1,2,0:T(8,128)(2,1)S(1)} %copy-done.7), kind=kOutput, calls=%fused_computation.1 | convolution fusion | flops 365977600 | bytes 23113728 | tf_op jit(solution)/shard_map/zgt,gtb->zb/dot_general | solution.py:146
  192.1 12.6 %all_to_all.25 = bf16[128,4,7168]{2,1,0:T(4,128)(2,1)} reshape(bf16[512,7168]{1,0:T(8,128)(2,1)} %fusion) | data formatting | bytes 14680064 | tf_op jit(solution)/shard_map/all_to_all | solution.py:153
  204.7 9.0 %all-to-all-start.2 = ((bf16[128,4,7168]{2,1,0:T(4,128)(2,1)}), bf16[128,4,7168]{2,1,0:T(4,128)(2,1)}, u32[]{:S(2)}, u32[]{:S(2)}) async-start(bf16[128,4,7168]{2,1,0:T(4,128)(2,1)} %all_to_all.25), calls=%async_computation.2 | async-start | bytes 14680064 | tf_op jit(solution)/shard_map/all_to_all | solution.py:153
  213.8 0.0 all-gather.2.cloned.1.call-start
  213.8 0.7 all-gather.2.cloned.1.call-update
  214.5 0.0 all-reduce.3.cloned.1.call-start
  214.5 107.3 %all-gather.2.cloned.1.call-done = bf16[128,7168]{1,0:T(8,128)(2,1)} async-done(((bf16[8,7168]{1,0:T(8,128)(2,1)}), bf16[128,7168]{1,0:T(8,128)(2,1)}) %all-gather.2.cloned.1.call-update) | async-done | bytes 1835024 | tf_op jit(solution)/shard_map/all_gather | solution.py:42
  321.8 2.7 fusion.35
  324.5 0.0 copy-start.13
  324.5 4.5 %convolution_convert_fusion = bf16[128,7168]{1,0:T(8,128)(2,1)} fusion(bf16[128,7168]{1,0:T(8,128)(2,1)S(1)} %copy-done, bf16[128,7168]{1,0:T(8,128)(2,1)} %all-gather.2.cloned.1.call-done, bf16[7168,128]{1,0:T(8,128)(2,1)} %param.22, f32[128,128]{1,0:T(8,128)S(1)} %fusion.35), kind=kOutput, calls=%fused_computation.5 | convolution fusion | flops 470777856 | bytes 7405568 | tf_op jit(solution)/shard_map/dot_general | solution.py:47
  329.0 0.0 all-reduce.3.cloned.1.call-update
  329.1 0.0 copy-done.13
  329.1 0.6 dynamic-slice
  330.3 0.0 all-to-all-done.2
  330.3 6.3 %bitcast_reduce_fusion = bf16[8,4,7168]{2,1,0:T(4,128)(2,1)S(1)} fusion(bf16[128,4,7168]{2,1,0:T(4,128)(2,1)} %all-to-all-done.2), kind=kLoop, calls=%fused_computation.10 | loop fusion | flops 3440640 | bytes 7798784 | tf_op jit(solution)/shard_map/reduce_sum | solution.py:156
  336.6 81.5 %all-reduce.3.cloned.1.call-done = bf16[128,7168]{1,0:T(8,128)(2,1)} async-done(((bf16[128,7168]{1,0:T(8,128)(2,1)}), bf16[128,7168]{1,0:T(8,128)(2,1)}) %all-reduce.3.cloned.1.call-update) | async-done | bytes 1835024
  418.2 2.0 fusion.2
  (32 shorter events, 0.2 us)
Async XLA Ops:
  6.5 318.0 %copy-start = (bf16[128,7168]{1,0:T(8,128)(2,1)S(1)}, bf16[128,7168]{1,0:T(8,128)(2,1)}, u32[]{:S(2)}) copy-start(bf16[128,7168]{1,0:T(8,128)(2,1)} %param.23) | copy-start | bytes 5505028
  7.5 14.0 %copy-start.5 = (pred[8,4,8]{0,2,1:T(8,128)(4,1)}, pred[8,4,8]{0,2,1:T(8,128)(4,1)S(1)}, u32[]{:S(2)}) copy-start(pred[8,4,8]{0,2,1:T(8,128)(4,1)S(1)} %fusion.29) | copy-start | bytes 772
  10.0 21.7 %all-to-all-start.1 = ((bf16[128,4,3]{1,2,0:T(4,128)(2,1)}), bf16[128,4,3]{1,2,0:T(4,128)(2,1)S(1)}, u32[]{:S(2)}, u32[]{:S(2)}) async-start(bf16[128,4,3]{1,2,0:T(4,128)(2,1)} %bitcast.21), calls=%async_computation.1 | async-start | bytes 262144 | tf_op jit(solution)/shard_map/all_to_all | solution.py:102
  37.0 94.4 %all-to-all-start = ((bf16[128,4,7168]{2,1,0:T(4,128)(2,1)}), bf16[128,4,7168]{2,1,0:T(4,128)(2,1)}, u32[]{:S(2)}, u32[]{:S(2)}) async-start(bf16[128,4,7168]{2,1,0:T(4,128)(2,1)} %bitcast.129), calls=%async_computation | async-start | bytes 14680064 | tf_op jit(solution)/shard_map/all_to_all | solution.py:101
  42.0 8.3 %copy-start.10 = (f32[3,56,1]{1,2,0:T(1,128)S(1)}, f32[3,56,1]{1,2,0:T(1,128)}, u32[]{:S(2)}) copy-start(f32[3,56,1]{1,2,0:T(1,128)} %param.28) | copy-start | bytes 2020
  50.4 8.3 %copy-start.11 = (f32[3,56,1]{1,2,0:T(1,128)S(1)}, f32[3,56,1]{1,2,0:T(1,128)}, u32[]{:S(2)}) copy-start(f32[3,56,1]{1,2,0:T(1,128)} %param.27) | copy-start | bytes 2020
  50.4 8.4 %copy-start.12 = (f32[3,1,56]{2,1,0:T(1,128)S(1)}, f32[3,1,56]{2,1,0:T(1,128)}, u32[]{:S(2)}) copy-start(f32[3,1,56]{2,1,0:T(1,128)} %param.29) | copy-start | bytes 2020
  131.4 21.0 %slice-start.2 = ((s8[5505024]{0:T(1024)(128)(4,1)}), s8[1310720]{0:T(1024)(128)(4,1)S(1)}, s32[]{:S(2)}) async-start(s8[5505024]{0:T(1024)(128)(4,1)} %bitcast.132), calls=%async_computation.7 | async-start | bytes 2621440
  143.6 8.8 %copy-start.1 = (bf16[512,7168,1]{1,0,2:T(8,128)(2,1)S(1)}, bf16[512,7168,1]{1,0,2:T(8,128)(2,1)}, u32[]{:S(2)}) copy-start(bf16[512,7168,1]{1,0,2:T(8,128)(2,1)} %reshape.80) | copy-start | bytes 22020100
  143.6 8.8 %slice-start.3 = ((s8[5505024]{0:T(1024)(128)(4,1)}), s8[4194304]{0:T(1024)(128)(4,1)S(1)}, s32[]{:S(2)}) async-start(s8[5505024]{0:T(1024)(128)(4,1)} %bitcast.132), calls=%async_computation.8 | async-start | bytes 8388608
  157.5 12.2 %copy-start.2 = (bf16[3,7168,32]{1,2,0:T(8,128)(2,1)S(1)}, bf16[3,7168,32]{1,2,0:T(8,128)(2,1)}, u32[]{:S(2)}) copy-start(bf16[3,7168,32]{1,2,0:T(8,128)(2,1)} %param.30) | copy-start | bytes 4128772
  169.7 5.7 %copy-start.3 = (f32[512,3,128]{2,0,1:T(8,128)S(1)}, f32[512,3,128]{2,0,1:T(8,128)}, u32[]{:S(2)}) copy-start(f32[512,3,128]{2,0,1:T(8,128)} %fusion.4) | copy-start | bytes 2359300
  169.7 5.7 %copy-start.9 = (bf16[3,2,16,128]{3,2,1,0:T(8,128)(2,1)S(1)}, bf16[3,2,16,128]{3,2,1,0:T(8,128)(2,1)}, u32[]{:S(2)}) copy-start(bf16[3,2,16,128]{3,2,1,0:T(8,128)(2,1)} %param.31) | copy-start | bytes 73732
  169.7 6.0 %copy-start.8 = (f32[512,3]{0,1:T(4,128)S(1)}, f32[512,3]{0,1:T(4,128)}, u32[]{:S(2)}) copy-start(f32[512,3]{0,1:T(4,128)} %reshape.78) | copy-start | bytes 18436
  169.7 6.0 %copy-start.14 = (f32[512,3,128]{2,0,1:T(8,128)S(1)}, f32[512,3,128]{2,0,1:T(8,128)}, u32[]{:S(2)}) copy-start(f32[512,3,128]{2,0,1:T(8,128)} %fusion.7) | copy-start | bytes 2359300
  169.7 6.5 %slice-start = ((s8[5505024]{0:T(1024)(128)(4,1)}), s8[4194304]{0:T(1024)(128)(4,1)S(1)}, s32[]{:S(2)}) async-start(s8[5505024]{0:T(1024)(128)(4,1)} %bitcast.130), calls=%async_computation.5 | async-start | bytes 8388608
  169.8 6.5 %slice-start.1 = ((s8[5505024]{0:T(1024)(128)(4,1)}), s8[1310720]{0:T(1024)(128)(4,1)S(1)}, s32[]{:S(2)}) async-start(s8[5505024]{0:T(1024)(128)(4,1)} %bitcast.130), calls=%async_computation.6 | async-start | bytes 2621440
  176.3 7.3 %copy-start.4 = (bf16[3,16,7168]{2,1,0:T(8,128)(2,1)S(1)}, bf16[3,16,7168]{2,1,0:T(8,128)(2,1)}, u32[]{:S(2)}) copy-start(bf16[3,16,7168]{2,1,0:T(8,128)(2,1)} %param.33) | copy-start | bytes 2064388
  176.3 7.2 %copy-start.7 = (bf16[3,128,16]{1,2,0:T(8,128)(2,1)S(1)}, bf16[3,128,16]{1,2,0:T(8,128)(2,1)}, u32[]{:S(2)}) copy-start(bf16[3,128,16]{1,2,0:T(8,128)(2,1)} %param.32) | copy-start | bytes 36868
  204.7 125.6 %all-to-all-start.2 = ((bf16[128,4,7168]{2,1,0:T(4,128)(2,1)}), bf16[128,4,7168]{2,1,0:T(4,128)(2,1)}, u32[]{:S(2)}, u32[]{:S(2)}) async-start(bf16[128,4,7168]{2,1,0:T(4,128)(2,1)} %all_to_all.25), calls=%async_computation.2 | async-start | bytes 14680064 | tf_op jit(solution)/shard_map/all_to_all | solution.py:153
  213.8 108.0 %all-gather.2.cloned.1.call-start = ((), (), s32[]{:S(2)}) async-start(), calls=%async_computation.3 | async-start | bytes 1949696 | tf_op jit(solution)/shard_map/all_gather | solution.py:42
  214.5 203.7 %all-reduce.3.cloned.1.call-start = ((), (), s32[]{:S(2)}) async-start(), calls=%async_computation.4 | async-start | bytes 3670016
  324.5 4.6 %copy-start.13 = (u32[128]{0:T(128)S(1)}, u32[128]{0:T(128)}, u32[]{:S(2)}) copy-start(u32[128]{0:T(128)} %constant.33) | copy-start | bytes 1540
  329.0 89.1 %copy-start.6 = (pred[8,4,8]{0,2,1:T(8,128)(4,1)S(1)}, pred[8,4,8]{0,2,1:T(8,128)(4,1)}, u32[]{:S(2)}) copy-start(pred[8,4,8]{0,2,1:T(8,128)(4,1)} %copy-done.5) | copy-start | bytes 772
Sparse Core Ops, SparseCore 0:
  216.7 105.0 all-gather.1
  329.2 88.9 all-reduce.2
where the time goes:
time: 429 us; the launch traced here: 427 us
  waiting for transfers between devices  269 us (63%)
  local copies, waits for them, and re-layouts  62.2 us (14%)
  matrix products  46.6 us (11%)
  starting transfers between devices  25.6 us (6%)
  between operations  14.4 us (3%)
  other arithmetic  8.72 us (2%)
    all_gather x1, waiting for transfers between devices, on_device(): shard_rows = lax.all_gather(tokens, 'local', axis=0, tiled=True)  107 us
    unnamed x3, waiting for transfers between devices  82.2 us
    all_to_all x1, waiting for transfers between devices, on_device(): lax.all_to_all(send_rows, ('group', 'local'), split_axis=0, concat_axis=0...  71.3 us
    all_to_all x2, local copies, waits for them, and re-layouts, on_device(): lax.all_to_all(send_rows, ('group', 'local'), split_axis=0, concat_axis=0...  24.4 us
    unnamed x50, local copies, waits for them, and re-layouts  17.6 us
    all_to_all x1, local copies, waits for them, and re-layouts, on_device(): lax.all_to_all(partials, ('group', 'local'), split_axis=0, concat_axis=0,...  12.6 us
    all_to_all x1, starting transfers between devices, on_device(): lax.all_to_all(send_weights, ('group', 'local'), split_axis=0, concat_axi...  11.5 us
    all_to_all x1, starting transfers between devices, on_device(): lax.all_to_all(partials, ('group', 'local'), split_axis=0, concat_axis=0,...  9.02 us
  transfers between devices with their start and end apart: 5, of which 4 were waited for; matrix products, arithmetic and copies ran while one was open for 8% of the time, Pallas kernels for 0%

commit v1 on v0

v1 whole, which is shorter than its diff:
```python
import functools

import jax
import jax.numpy as jnp
from jax import lax
from jax.experimental import pallas as pl
from jax.experimental.pallas import tpu as pltpu
from jax.sharding import PartitionSpec as P

MESH = pl.DeviceIdType.MESH
F32 = jnp.float32
BF16 = jnp.bfloat16

WIDTH = 7168
HALF = WIDTH // 2
SIDE = 4
ROWS = 16
QB = 128
LANES = 128
HID = 384
GU = 2 * HID
DOWN = HID + LANES

UNITS = (
    ((0, 1, 2), 0, 768),
    ((1, 2, 0), 768, 768),
    ((2, 0, 1), 1536, 512),
    ((0, 1, 2), 2048, 512),
    ((1, 2, 0), 2560, 512),
    ((2, 0, 1), 3072, 512),
)
NU = len(UNITS)
PICK_UNIT = 2
EARLY = (0, 1, 2)
LATE = (3, 4, 5)


def gathered_width(u):
    return UNITS[u][2] + (LANES if u == PICK_UNIT else 0)


def cut_of(width):
    return (width // 256) * LANES


def halved(cols, h):
    if h is None:
        return pl.ds(0, cols)
    cut = cut_of(cols)
    return pl.ds(0, cut) if h == 0 else pl.ds(cut, cols - cut)


def slab(order, k, q, own, h, cols):
    ix = [None] * 3
    for j, a in enumerate(order):
        ix[a] = pl.ds(0, SIDE) if j < k else (q if j == k else own[a])
    if k == 0:
        return (*ix, pl.ds(0, ROWS), halved(cols, h))
    if h is not None:
        ix[order[0]] = pl.ds(2 * h, 2)
    return (*ix, pl.ds(0, ROWS), pl.ds(0, cols))


def landing(slot, order, k, h, cols):
    if k == 0:
        return (slot, pl.ds(0, ROWS), halved(cols, h))
    whole = sorted(order[:k])
    ix = [pl.ds(0, SIDE)] * k
    if h is not None:
        ix[whole.index(order[0])] = pl.ds(2 * h, 2)
    return (slot, *ix, pl.ds(0, ROWS), pl.ds(0, cols))


def dot(a, b):
    return jnp.dot(a, b, preferred_element_type=F32)


def dot_t(a, b):
    return lax.dot_general(a, b, (((0,), (0,)), ((), ())), preferred_element_type=F32)


def kernel(*refs):
    it = iter(refs)

    def take(n):
        return [next(it) for _ in range(n)]

    (scales, tokens, picked, weight, out_maps, a_t) = take(6)
    (gate_w, up_w, down_w, sgate_w, sup_w, sdown_w, in_t, b_maps) = take(8)
    (out,) = take(1)
    G = take(NU)
    O = take(NU)
    S = take(NU)
    R = [take(3) for _ in range(NU)]
    (gu, sgu, dcat, in_v, b_v, acc, acc_s, hcat, out_bd, a_bd, xs, xf, fs, fr) = take(14)
    (w_sem, m_sem, x_sem, ag_s, ag_r, as_s, as_r, rs_s, rs_r, ss_s, ss_r) = take(11)

    g = lax.axis_index("group")
    loc = lax.axis_index("local")
    x, c = g // 2, g % 2
    z, y = loc // SIDE, loc % SIDE
    own = (x, y, z)
    o = 1 - c

    def along(axis, step):
        p = (own[axis] + step + SIDE) % SIDE
        if axis == 0:
            return (p * 2 + c, loc)
        if axis == 1:
            return (g, z * SIDE + p)
        return (g, p * SIDE + y)

    sibling = (x * 2 + o, loc)

    def at(axis, step):
        return (own[axis] + step + SIDE) % SIDE

    def remote(src, dst, ss, rs, dev):
        return pltpu.make_async_remote_copy(
            src_ref=src, dst_ref=dst, send_sem=ss, recv_sem=rs, device_id=dev, device_id_type=MESH
        )

    quarter = WIDTH // 4
    mine0 = c * HALF
    other0 = o * HALF
    starts = (mine0, mine0 + quarter, other0, other0 + quarter)

    def w_copy(i, j):
        src = (gate_w if j < 3 else up_w).at[j % 3, pl.ds(starts[i], quarter)]
        return pltpu.make_async_copy(src, gu.at[pl.ds(starts[i], quarter), pl.ds(j * LANES, LANES)], w_sem.at[i, j])

    m_copies = [
        pltpu.make_async_copy(in_t, in_v, m_sem.at[0]),
        pltpu.make_async_copy(sgate_w, sgu.at[:, pl.ds(0, LANES)], m_sem.at[1]),
        pltpu.make_async_copy(sup_w, sgu.at[:, pl.ds(LANES, LANES)], m_sem.at[2]),
        pltpu.make_async_copy(b_maps, b_v, m_sem.at[3]),
        pltpu.make_async_copy(sdown_w, dcat.at[pl.ds(HID, LANES)], m_sem.at[4]),
    ] + [
        pltpu.make_async_copy(down_w.at[e], dcat.at[pl.ds(e * LANES, LANES)], m_sem.at[5 + e]) for e in range(3)
    ]
    m_copies[0].start()
    for i in range(4):
        for j in range(6):
            w_copy(i, j).start()
    for m in m_copies[1:]:
        m.start()

    barrier = pltpu.get_barrier_semaphore()
    partners = [along(a, s) for a in range(3) for s in (1, -1)] + [sibling]
    for p in partners:
        pl.semaphore_signal(barrier, inc=1, device_id=p, device_id_type=MESH)

    lane = lax.broadcasted_iota(jnp.int32, (8, LANES), 1)
    pick = jnp.zeros((8, LANES), F32)
    for k in range(8):
        pick = pick + jnp.where(lane == picked[:, k : k + 1], weight[:, k : k + 1].astype(F32), 0.0)
    xs[:, pl.ds(0, HALF)] = tokens[:, pl.ds(pl.multiple_of(other0, LANES), HALF)].astype(F32)
    xs[:, pl.ds(HALF, LANES)] = pick
    xf[c, :, pl.ds(0, HALF)] = tokens[:, pl.ds(pl.multiple_of(mine0, LANES), HALF)].astype(F32)
    xf[c, :, pl.ds(HALF, LANES)] = pick
    pl.semaphore_wait(barrier, len(partners))
    swap = remote(xs, xf.at[c], x_sem.at[0], x_sem.at[1], sibling)
    swap.start()

    out_bd[...] = jnp.zeros_like(out_bd)
    a_bd[...] = jnp.zeros_like(a_bd)
    for e in range(3):
        for h in range(2):
            out_bd[pl.ds(e * 32 + h * 16, 16), pl.ds((h * 3 + e) * LANES, LANES)] = out_maps[e, h]
        a_bd[pl.ds(e * 16, 16), pl.ds(e * LANES, LANES)] = a_t[e]
    hcat[:, :, :, :, pl.ds(HID, LANES)] = jnp.zeros((SIDE, SIDE, SIDE, ROWS, LANES), BF16)

    swap.wait_send()
    remote(xs, xf.at[o], x_sem.at[0], x_sem.at[1], sibling).wait_recv()
    block = xf[...].reshape(ROWS, HALF + LANES).astype(BF16)
    for u, (order, first, cols) in enumerate(UNITS):
        G[u][x, y, z, :, pl.ds(0, cols)] = block[:, first : first + cols]
        if u == PICK_UNIT:
            G[u][x, y, z, :, pl.ds(cols, LANES)] = block[:, HALF:]

    def ag(u, k, which, arriving=False):
        order = UNITS[u][0]
        a = order[k]
        w = gathered_width(u)
        step = 1 if which in (0, 2) else -1
        if which < 2:
            sent, got, h = at(a, 0), at(a, -step), None
        else:
            sent, got, h = at(a, -step), at(a, -2 * step), which - 2
        part = G[u].at[slab(order, k, got if arriving else sent, own, h, w)]
        return remote(part, part, ag_s.at[u, k, which], ag_r.at[u, k, which], along(a, step))

    def ag_open(u, k):
        for which in (0, 1):
            ag(u, k, which).start()

    def ag_forward(u, k):
        for which in (0, 1):
            ag(u, k, which, True).wait_recv()
            ag(u, k, which + 2).start()

    def ag_close(u, k):
        for which in (2, 3):
            ag(u, k, which, True).wait_recv()

    QUARTER = (0, -1, 1, 2)

    def hand(u, i):
        order, _, cols = UNITS[u]
        at_q = slab(order, 2, at(order[2], QUARTER[i]), own, None, cols)
        return remote(G[u].at[at_q], O[u].at[at_q], as_s.at[u, i], as_r.at[u, i], sibling)

    def gate_up(u, i, src, first0):
        order, first, cols = UNITS[u]
        at_q = slab(order, 2, at(order[2], QUARTER[i]), own, None, cols)
        at_a = slab(order, 2, at(order[2], QUARTER[i]), own, None, GU)
        rows = pl.ds(pl.multiple_of(first0 + first, LANES), cols)
        got = dot(src[at_q].reshape(256, cols), gu[rows, :]).reshape(SIDE, SIDE, ROWS, GU)
        acc[at_a] = acc[at_a] + got

    def shared(u, src, first0):
        _, first, cols = UNITS[u]
        rows = pl.ds(pl.multiple_of(first0 + first, LANES), cols)
        acc_s[...] += dot(src[x, pl.ds(2 * c, 2), :, :, pl.ds(0, cols)].reshape(128, cols), sgu[rows, :])

    def merge_up(k0, n):
        def body(i, carry):
            kb = k0 + i
            ks = pl.ds(pl.multiple_of(kb * QB, QB), QB)
            ab = dot_t(in_v[:, :, ks].reshape(96, QB), out_bd[...])
            for j in range(6):
                cs = pl.ds(j * LANES, LANES)
                s = scales[j * 56 + kb]
                gu[ks, cs] = (gu[ks, cs].astype(F32) * s + ab[:, j * LANES : (j + 1) * LANES]).astype(BF16)
            return carry

        lax.fori_loop(0, n, body, 0)

    def merge_down():
        def body(i, carry):
            ns = pl.ds(pl.multiple_of(i * 256, 256), 256)
            ab = dot_t(a_bd[...], b_v[:, :, ns].reshape(48, 256))
            for e in range(3):
                for t in range(2):
                    at_d = (pl.ds(e * LANES, LANES), pl.ds(pl.multiple_of(i * 256 + t * 128, 128), 128))
                    s = scales[336 + e * 56 + i * 2 + t]
                    part = ab[e * 128 : (e + 1) * 128, t * 128 : (t + 1) * 128]
                    dcat[at_d] = (dcat[at_d].astype(F32) * s + part).astype(BF16)
            return carry

        lax.fori_loop(0, WIDTH // 256, body, 0)

    def wait_w(i):
        for j in range(6):
            w_copy(i, j).wait()

    ALL = EARLY + LATE
    for u in ALL:
        ag_open(u, 0)
    acc[...] = jnp.zeros_like(acc)
    acc_s[...] = jnp.zeros_like(acc_s)
    m_copies[0].wait()
    wait_w(0)
    for u in ALL:
        ag_forward(u, 0)
    merge_up(c * 28, 7)
    for u in ALL:
        ag_close(u, 0)
        ag_open(u, 1)
    merge_up(c * 28 + 7, 7)
    wait_w(1)
    for u in ALL:
        ag_forward(u, 1)
    merge_up(c * 28 + 14, 14)
    for u in ALL:
        ag_close(u, 1)
        ag_open(u, 2)
        hand(u, 0).start()
    for u in EARLY:
        gate_up(u, 0, G[u], mine0)
    wait_w(2)
    wait_w(3)
    merge_up(o * 28, 28)
    for u in EARLY:
        hand(u, 0).wait_recv()
        gate_up(u, 0, O[u], other0)
    for u in EARLY:
        ag_forward(u, 2)
        hand(u, 1).start()
        hand(u, 2).start()
    for u in LATE:
        gate_up(u, 0, G[u], mine0)
        hand(u, 0).wait_recv()
        gate_up(u, 0, O[u], other0)
    for u in EARLY:
        gate_up(u, 1, G[u], mine0)
        gate_up(u, 2, G[u], mine0)
        hand(u, 1).wait_recv()
        gate_up(u, 1, O[u], other0)
        hand(u, 2).wait_recv()
        gate_up(u, 2, O[u], other0)
    for u in LATE:
        ag_forward(u, 2)
        hand(u, 1).start()
        hand(u, 2).start()
    for m in m_copies[1:]:
        m.wait()
    merge_down()
    for u in EARLY:
        ag_close(u, 2)
        hand(u, 3).start()
    for u in LATE:
        gate_up(u, 1, G[u], mine0)
        gate_up(u, 2, G[u], mine0)
        hand(u, 1).wait_recv()
        gate_up(u, 1, O[u], other0)
        hand(u, 2).wait_recv()
        gate_up(u, 2, O[u], other0)
    for u in EARLY:
        gate_up(u, 3, G[u], mine0)
        shared(u, G[u], mine0)
        hand(u, 3).wait_recv()
        gate_up(u, 3, O[u], other0)
        shared(u, O[u], other0)
    for u in LATE:
        ag_close(u, 2)
        hand(u, 3).start()
    for u in LATE:
        gate_up(u, 3, G[u], mine0)
        shared(u, G[u], mine0)
    for u in LATE:
        hand(u, 3).wait_recv()
        gate_up(u, 3, O[u], other0)
        shared(u, O[u], other0)

    choose = (
        lax.broadcasted_iota(jnp.int32, (LANES, HID), 0)
        == lax.broadcasted_iota(jnp.int32, (LANES, HID), 1) // LANES + g * 3
    ).astype(BF16)
    pick_cols = pl.ds(UNITS[PICK_UNIT][2], LANES)

    def activate(i, carry):
        xi, yi = i // SIDE, i % SIDE
        gate = acc[xi, yi, :, :, pl.ds(0, HID)].reshape(64, HID)
        up = acc[xi, yi, :, :, pl.ds(HID, HID)].reshape(64, HID)
        picks = dot(G[PICK_UNIT][xi, yi, :, :, pick_cols].reshape(64, LANES), choose)
        hidden = (gate / (1.0 + jnp.exp(-gate)) * up * picks).astype(BF16)
        hcat[xi, yi, :, :, pl.ds(0, HID)] = hidden.reshape(SIDE, ROWS, HID)
        return carry

    lax.fori_loop(0, SIDE * SIDE, activate, 0)
    sg = acc_s[:, pl.ds(0, LANES)]
    su = acc_s[:, pl.ds(LANES, LANES)]
    hcat[x, pl.ds(2 * c, 2), :, :, pl.ds(HID, LANES)] = (
        (sg / (1.0 + jnp.exp(-sg)) * su).astype(BF16).reshape(2, SIDE, ROWS, LANES)
    )

    for u in ALL:
        for k in range(3):
            for which in range(4):
                ag(u, k, which).wait_send()
        for i in range(4):
            hand(u, i).wait_send()

    def rows_of(u, i):
        order = UNITS[u][0]
        at_h = slab(order, 2, at(order[2], QUARTER[i]), own, None, DOWN)
        return hcat[at_h].reshape(256, DOWN)

    def give(u, i):
        order, _, cols = UNITS[u]
        at_q = slab(order, 2, at(order[2], QUARTER[i]), own, None, cols)
        return remote(O[u].at[at_q], S[u].at[at_q], ss_s.at[u, i], ss_r.at[u, i], sibling)

    def down_other(u, i):
        order, first, cols = UNITS[u]
        at_q = slab(order, 2, at(order[2], QUARTER[i]), own, None, cols)
        ns = pl.ds(pl.multiple_of(other0 + first, LANES), cols)
        O[u][at_q] = dot(rows_of(u, i), dcat[:, ns]).astype(BF16).reshape(SIDE, SIDE, ROWS, cols)
        give(u, i).start()

    def down_mine(u, i):
        order, first, cols = UNITS[u]
        at_q = slab(order, 2, at(order[2], QUARTER[i]), own, None, cols)
        ns = pl.ds(pl.multiple_of(mine0 + first, LANES), cols)
        mine = dot(rows_of(u, i), dcat[:, ns]).reshape(SIDE, SIDE, ROWS, cols)
        give(u, i).wait_recv()
        G[u][at_q] = (mine + S[u][at_q].astype(F32)).astype(BF16)

    def rs(u, k, which):
        order, _, cols = UNITS[u]
        a = order[k]
        right = which % 2 == 0
        step = 1 if right else -1
        if which < 2:
            q, h, slot = at(a, 2), which, 0
        elif which < 4:
            q, h, slot = at(a, step), (1 if right else 0), (1 if right else 2)
        else:
            q, h, slot = at(a, step), (0 if right else 1), (1 if right else 2)
        src = G[u].at[slab(order, k, q, own, h, cols)]
        dst = R[u][k].at[landing(slot, order, k, h, cols)]
        return remote(src, dst, rs_s.at[u, k, which], rs_r.at[u, k, which], along(a, step))

    def rs_far(u, k):
        rs(u, k, 0).start()
        rs(u, k, 1).start()

    def rs_near(u, k, which):
        rs(u, k, which).start()

    def rs_pass(u, k):
        order, _, cols = UNITS[u]
        a = order[k]
        for which in (0, 1):
            step = 1 if which == 0 else -1
            rs(u, k, which).wait_recv()
            at_q = slab(order, k, at(a, step), own, which, cols)
            came = R[u][k][landing(0, order, k, which, cols)]
            G[u][at_q] = (G[u][at_q].astype(F32) + came.astype(F32)).astype(BF16)
            rs(u, k, 4 + which).start()

    def rs_sum(u, k):
        order, _, cols = UNITS[u]
        for which in (2, 3, 4, 5):
            rs(u, k, which).wait_recv()
        at_q = slab(order, k, own[order[k]], own, None, cols)
        l = R[u][k][landing(1, order, k, None, cols)]
        r = R[u][k][landing(2, order, k, None, cols)]
        return at_q, G[u][at_q].astype(F32) + (l.astype(F32) + r.astype(F32))

    def rs_next(u, k):
        at_q, total = rs_sum(u, k)
        G[u][at_q] = total.astype(BF16)
        rs_far(u, k - 1)
        rs_near(u, k - 1, 2)
        rs_near(u, k - 1, 3)

    def first_half(us):
        for u in us:
            down_other(u, 3)
        for u in us:
            down_other(u, 2)
        for u in us:
            down_mine(u, 3)
            rs_far(u, 2)
        for u in us:
            down_other(u, 1)
        for u in us:
            down_mine(u, 2)
            rs_near(u, 2, 2)
        for u in us:
            down_mine(u, 1)
            rs_near(u, 2, 3)

    first_half(EARLY)
    for u in EARLY:
        down_other(u, 0)
    first_half(LATE)
    for u in EARLY:
        rs_pass(u, 2)
    for u in LATE:
        down_other(u, 0)
    for u in EARLY:
        down_mine(u, 0)
    for u in LATE:
        rs_pass(u, 2)
    for u in LATE:
        down_mine(u, 0)
    for us in (EARLY, LATE):
        for u in us:
            rs_next(u, 2)
    for us in (EARLY, LATE):
        for u in us:
            rs_pass(u, 1)
    for us in (EARLY, LATE):
        for u in us:
            rs_next(u, 1)
    for us in (EARLY, LATE):
        for u in us:
            rs_pass(u, 0)
    for us in (EARLY, LATE):
        for u in us:
            _, first, cols = UNITS[u]
            _, total = rs_sum(u, 0)
            fs[:, :, pl.ds(first, cols)] = total.reshape(2, 8, cols)

    final = remote(fs.at[o], fr, x_sem.at[2], x_sem.at[3], sibling)
    final.start()
    out[:, pl.ds(pl.multiple_of(mine0, LANES), HALF)] = fs[c].astype(BF16)
    final.wait_recv()
    out[:, pl.ds(pl.multiple_of(other0, LANES), HALF)] = fr[...].astype(BF16)
    final.wait_send()
    for u in ALL:
        for k in range(3):
            for which in range(6):
                rs(u, k, which).wait_send()
        for i in range(4):
            give(u, i).wait_send()


def on_device(
    tokens,
    picked_group_index,
    picked_expert_index,
    routing_pick_weight,
    common_gate_weight,
    common_up_weight,
    common_down_weight,
    routed_gate_weight,
    routed_up_weight,
    routed_down_weight,
    gate_block_scales,
    up_block_scales,
    down_block_scales,
    adapter_input_maps,
    adapter_output_maps,
    adapter_down_input,
    adapter_down_output,
):
    scales = jnp.concatenate(
        [gate_block_scales.reshape(-1), up_block_scales.reshape(-1), down_block_scales.reshape(-1)]
    )
    vmem = pl.BlockSpec(memory_space=pltpu.VMEM)
    hbm = pl.BlockSpec(memory_space=pl.ANY)
    scratch = []
    for u, (_, _, cols) in enumerate(UNITS):
        scratch.append(pltpu.VMEM((SIDE, SIDE, SIDE, ROWS, gathered_width(u)), BF16))
    for _ in range(2):
        for _, _, cols in UNITS:
            scratch.append(pltpu.VMEM((SIDE, SIDE, SIDE, ROWS, cols), BF16))
    for _, _, cols in UNITS:
        for k in range(3):
            scratch.append(pltpu.VMEM((3, *([SIDE] * k), ROWS, cols), BF16))
    scratch += [
        pltpu.VMEM((WIDTH, GU), BF16),
        pltpu.VMEM((WIDTH, 2 * LANES), BF16),
        pltpu.VMEM((DOWN, WIDTH), BF16),
        pltpu.VMEM((3, 32, WIDTH), BF16),
        pltpu.VMEM((3, 16, WIDTH), BF16),
        pltpu.VMEM((SIDE, SIDE, SIDE, ROWS, GU), F32),
        pltpu.VMEM((128, 2 * LANES), F32),
        pltpu.VMEM((SIDE, SIDE, SIDE, ROWS, DOWN), BF16),
        pltpu.VMEM((96, GU), BF16),
        pltpu.VMEM((48, HID), BF16),
        pltpu.VMEM((8, HALF + LANES), F32),
        pltpu.VMEM((2, 8, HALF + LANES), F32),
        pltpu.VMEM((2, 8, HALF), F32),
        pltpu.VMEM((8, HALF), F32),
        pltpu.SemaphoreType.DMA((4, 6)),
        pltpu.SemaphoreType.DMA((8,)),
        pltpu.SemaphoreType.DMA((4,)),
        pltpu.SemaphoreType.DMA((NU, 3, 4)),
        pltpu.SemaphoreType.DMA((NU, 3, 4)),
        pltpu.SemaphoreType.DMA((NU, 4)),
        pltpu.SemaphoreType.DMA((NU, 4)),
        pltpu.SemaphoreType.DMA((NU, 3, 6)),
        pltpu.SemaphoreType.DMA((NU, 3, 6)),
        pltpu.SemaphoreType.DMA((NU, 4)),
        pltpu.SemaphoreType.DMA((NU, 4)),
    ]
    return pl.pallas_call(
        kernel,
        out_shape=jax.ShapeDtypeStruct((8, WIDTH), BF16),
        in_specs=[pl.BlockSpec(memory_space=pltpu.SMEM)] + [vmem] * 5 + [hbm] * 8,
        out_specs=vmem,
        scratch_shapes=scratch,
        compiler_params=pltpu.CompilerParams(
            collective_id=0, has_side_effects=True, vmem_limit_bytes=62 * 2**20
        ),
        cost_estimate=pl.CostEstimate(flops=22 * 10**9, bytes_accessed=25 * 10**6, transcendentals=10**6),
    )(
        scales,
        tokens,
        picked_expert_index,
        routing_pick_weight,
        adapter_output_maps,
        adapter_down_input.transpose(0, 2, 1),
        routed_gate_weight,
        routed_up_weight,
        routed_down_weight,
        common_gate_weight,
        common_up_weight,
        common_down_weight,
        adapter_input_maps.transpose(0, 2, 1),
        adapter_down_output,
    )


def solution(mesh):
    in_specs = (
        P(("group", "local"), None),
        P(("group", "local"), None),
        P(("group", "local"), None),
        P(("group", "local"), None),
        P(None, "local"),
        P(None, "local"),
        P("local", None),
        P("group", None, "local"),
        P("group", None, "local"),
        P("group", "local", None),
        P("group", None, "local"),
        P("group", None, "local"),
        P("group", "local", None),
        P("group", None, None),
        P("group", None, None, "local"),
        P("group", "local", None),
        P("group", None, None),
    )
    return jax.shard_map(
        on_device, mesh=mesh, in_specs=in_specs, out_specs=P(("group", "local"), None), check_vma=False
    )
```

time: 429 us -> 117 us (0.27)
  waiting for transfers between devices: 269 us -> 0 us
  Pallas kernels: 0 us -> 112 us
  local copies, waits for them, and re-layouts: 62.2 us -> 1.81 us
  matrix products: 46.6 us -> 0 us
  starting transfers between devices: 25.6 us -> 0 us
  between operations: 14.4 us -> 0.01 us
  other arithmetic: 8.72 us -> 2.76 us
    pallas_call x0 -> x1, Pallas kernels: none -> 112 us  [on_device(): pl.pallas_call(kernel, out_shape=jax.ShapeDtypeStruct((8, WIDTH), BF16),...]
    all_gather x1 -> x0, waiting for transfers between devices: 107 us -> none  [on_device(): shard_rows = lax.all_gather(tokens, 'local', axis=0, tiled=True)]
    unnamed x3 -> x0, waiting for transfers between devices: 82.2 us -> none
    all_to_all x3 -> x0, waiting for transfers between devices: 80 us -> none  [the longest x1 71.3 us: on_device(): lax.all_to_all(send_rows, ('group', 'local'), split_axis=0, concat_axis=0...]
    dot_general x12 -> x0, matrix products: 46.6 us -> none  [the longest x1 8.75 us: on_device(): jnp.dot(arrived_rows, up_cat, preferred_element_type=jnp.float32)]
    all_to_all x4 -> x0, local copies, waits for them, and re-layouts: 37.2 us -> none  [the longest x2 24.4 us: on_device(): lax.all_to_all(send_rows, ('group', 'local'), split_axis=0, concat_axis=0...]
    all_to_all x3 -> x0, starting transfers between devices: 25.5 us -> none  [the longest x1 11.5 us: on_device(): lax.all_to_all(send_weights, ('group', 'local'), split_axis=0, concat_axi...]
    unnamed x50 -> x1, local copies, waits for them, and re-layouts: 17.6 us -> 1.55 us
  transfers between devices with their start and end apart: 5 -> 0, of which waited for: 4 -> 0; matrix products, arithmetic and copies ran while one was open for 8% -> 0% of each run, Pallas kernels for 0% -> 0%
where the time goes in v1:
time: 117 us
  Pallas kernels  112 us (96%)
  other arithmetic  2.76 us (2%)
  local copies, waits for them, and re-layouts  1.81 us (2%)
    pallas_call x1, Pallas kernels, on_device(): pl.pallas_call(kernel, out_shape=jax.ShapeDtypeStruct((8, WIDTH), BF16),...  112 us

profile of v1, /device:TPU:1, one launch (start us, length us, event | category | flops | bytes accessed | tf_op | source)
XLA Modules:
  0.0 116.8 jit_solution(3625170253152718831)
XLA Ops:
  0.0 0.7 reduce
  0.7 0.1 reshape.9
  0.8 0.7 reduce.1
  1.5 0.1 reshape.10
  1.6 0.7 reduce.2
  2.3 0.1 reshape.11
  2.4 0.7 pad_maximum_fusion.refs_0_
  3.0 112.2 %shard_map.154 = bf16[8,7168]{1,0:T(8,128)(2,1)} custom-call(f32[504]{0:T(512)} %pad_maximum_fusion.refs_0_, bf16[8,7168]{1,0:T(8,128)(2,1)} %refs_1_.1, s32[8,8]{1,0:T(8,128)} %refs_2_.1, bf16[8,8]{1,0:T(8,128)(2,1)} %refs_3_.1, bf16[3,2,16,128]{3,2,1,0:T(8,128)(2,1)} %refs_4_.1, bf16[3,16,128]{2,1,0:T(8,128)(2,1)} %bitcast.3, ...), custom_call_target="tpu_custom_call" | custom-call | flops 22000001024 | bytes 25000000 | tf_op jit(solution)/shard_map/pallas_call | solution.py:562
  115.2 1.6 %copy.18 = bf16[8,7168]{1,0:T(8,128)(2,1)} copy(bf16[8,7168]{1,0:T(8,128)(2,1)} %shard_map.154) | data formatting | bytes 229376

commit v2 on v1

v2 whole, which is shorter than its diff:
```python
import functools

import jax
import jax.numpy as jnp
from jax import lax
from jax.experimental import pallas as pl
from jax.experimental.pallas import tpu as pltpu
from jax.sharding import PartitionSpec as P

MESH = pl.DeviceIdType.MESH
F32 = jnp.float32
BF16 = jnp.bfloat16

WIDTH = 7168
HALF = WIDTH // 2
SIDE = 4
ROWS = 16
QB = 128
LANES = 128
HID = 384
GU = 2 * HID
DOWN = HID + LANES

UNITS = (
    ((0, 1, 2), 0, 1280),
    ((1, 2, 0), 1280, 1280),
    ((2, 0, 1), 2560, 1024),
)
NU = len(UNITS)
PICK_UNIT = 2
REL = (0, 1, -1, 2)

AG_GROUPS = (
    ((0, 0, 0),),
    ((0, 0, 1),),
    ((0, 0, 2), (0, 1, 2)),
    ((1, 0, 0), (1, -1, 1)),
    ((1, 1, 0), (1, 2, 1)),
    ((1, -1, 0), (1, 2, 0)),
    ((1, 0, 1), (1, 1, 1)),
    ((1, 0, 2), (1, 1, 2), (1, -1, 2), (1, 2, 2)),
    ((2, 0, 0), (2, 0, 1)),
    ((2, -1, 0), (2, -1, 1)),
    ((2, 1, 0), (2, 1, 1)),
    ((2, 2, 0), (2, 2, 1)),
    ((2, 0, 2), (2, -1, 2)),
    ((2, 1, 2), (2, 2, 2)),
)
AG_WAITS = len(AG_GROUPS)
AG_GROUP_OF = {copy: i for i, group in enumerate(AG_GROUPS) for copy in group}
HERE = ((None, 0),)
NEAR_A = ((0, -1), (0, 1), (-1, -1), (-1, 1))
NEAR_B = ((1, -1), (1, 1), (2, -1), (2, 1))
FAR_A = ((0, 2), (-1, 2))
FAR_B = ((1, 2), (2, 2))
HAND_GROUPS = (HERE, NEAR_A, NEAR_B, FAR_A, FAR_B)


def gathered_width(u):
    return UNITS[u][2] + (LANES if u == PICK_UNIT else 0)


def halved(cols, h):
    if h is None:
        return pl.ds(0, cols)
    cut = cols // 256 * LANES
    return pl.ds(0, cut) if h == 0 else pl.ds(cut, cols - cut)


def landing(slot, order, k, piece, at, cols):
    if k == 0:
        return (slot, pl.ds(0, ROWS), halved(cols, piece))
    whole = sorted(order[:k])
    ix = [pl.ds(0, SIDE)] * k
    if piece is not None:
        ix[whole.index(order[k - 1])] = at(order[k - 1], piece)
    return (slot, *ix, pl.ds(0, ROWS), pl.ds(0, cols))


def dot(a, b):
    return jnp.dot(a, b, preferred_element_type=F32)


def dot_t(a, b):
    return lax.dot_general(a, b, (((0,), (0,)), ((), ())), preferred_element_type=F32)


def kernel(*refs):
    it = iter(refs)

    def take(n):
        return [next(it) for _ in range(n)]

    small_in = take(8)
    (gate_w, up_w, down_w, sgate_w, sup_w, sdown_w, in_t, b_maps) = take(8)
    (out,) = take(1)
    G = take(NU)
    O = take(NU)
    S = take(NU)
    R = [take(3) for _ in range(NU)]
    (gu, sgu, dcat, in_v, b_v, acc, acc_s, hcat, out_bd, a_bd, xs, xf, fs, fr) = take(14)
    small = take(8)
    (gate_s, up_s, down_s, tokens, picked, weight, out_maps, a_t) = small
    (i_sem, w_sem, m_sem, x_sem, ag_s, ag_r, as_s, as_r, rs_s, rs_r, ss_s, ss_r) = take(12)

    g = lax.axis_index("group")
    loc = lax.axis_index("local")
    x, c = g // 2, g % 2
    z, y = loc // SIDE, loc % SIDE
    own = (x, y, z)
    o = 1 - c

    def along(axis, step):
        p = (own[axis] + step + SIDE) % SIDE
        if axis == 0:
            return (p * 2 + c, loc)
        if axis == 1:
            return (g, z * SIDE + p)
        return (g, p * SIDE + y)

    sibling = (x * 2 + o, loc)

    def at(axis, step):
        return (own[axis] + step + SIDE) % SIDE

    def part(order, k, q, piece, cols):
        ix = list(own)
        for a in order[:k]:
            ix[a] = pl.ds(0, SIDE)
        ix[order[k]] = at(order[k], q)
        if k == 0:
            return (*ix, pl.ds(0, ROWS), halved(cols, piece))
        if piece is not None:
            ix[order[k - 1]] = at(order[k - 1], piece)
        return (*ix, pl.ds(0, ROWS), pl.ds(0, cols))

    def remote(src, dst, ss, rs, dev):
        return pltpu.make_async_remote_copy(
            src_ref=src, dst_ref=dst, send_sem=ss, recv_sem=rs, device_id=dev, device_id_type=MESH
        )

    barrier = pltpu.get_barrier_semaphore()
    partners = [along(a, s) for a in range(3) for s in (1, -1)] + [sibling]
    for p in partners:
        pl.semaphore_signal(barrier, inc=1, device_id=p, device_id_type=MESH)

    inward = [pltpu.make_async_copy(a, b, i_sem.at[i]) for i, (a, b) in enumerate(zip(small_in, small))]
    for i in (3, 4, 5, 6, 7, 0, 1, 2):
        inward[i].start()
    mine0 = c * HALF
    other0 = o * HALF
    w_rows = ((mine0, HALF // 2), (mine0 + HALF // 2, HALF // 2), (other0, HALF))

    def w_copy(i, j):
        rows = pl.ds(*w_rows[i])
        src = (gate_w if j < 3 else up_w).at[j % 3, rows]
        return pltpu.make_async_copy(src, gu.at[rows, pl.ds(j * LANES, LANES)], w_sem.at[i])

    def m_copy(i):
        if i == 0:
            return pltpu.make_async_copy(in_t, in_v, m_sem.at[0])
        if i < 3:
            src = sgate_w if i == 1 else sup_w
            return pltpu.make_async_copy(src, sgu.at[:, pl.ds((i - 1) * LANES, LANES)], m_sem.at[1])
        if i == 3:
            return pltpu.make_async_copy(b_maps, b_v, m_sem.at[2])
        if i == 4:
            return pltpu.make_async_copy(sdown_w, dcat.at[pl.ds(HID, LANES)], m_sem.at[3])
        return pltpu.make_async_copy(down_w.at[i - 5], dcat.at[pl.ds((i - 5) * LANES, LANES)], m_sem.at[3])

    def wait_all(ref, sem):
        pltpu.make_async_copy(ref, ref, sem).wait()

    m_copy(0).start()
    for j in range(6):
        w_copy(0, j).start()

    out_bd[...] = jnp.zeros_like(out_bd)
    a_bd[...] = jnp.zeros_like(a_bd)
    hcat[:, :, :, :, pl.ds(HID, LANES)] = jnp.zeros((SIDE, SIDE, SIDE, ROWS, LANES), BF16)
    for i in (3, 4, 5):
        inward[i].wait()
    lane = lax.broadcasted_iota(jnp.int32, (8, LANES), 1)
    pick = jnp.zeros((8, LANES), F32)
    for k in range(8):
        pick = pick + jnp.where(lane == picked[:, k : k + 1], weight[:, k : k + 1].astype(F32), 0.0)
    xs[:, pl.ds(0, HALF)] = tokens[:, pl.ds(pl.multiple_of(other0, LANES), HALF)].astype(F32)
    xs[:, pl.ds(HALF, LANES)] = pick
    xf[c, :, pl.ds(0, HALF)] = tokens[:, pl.ds(pl.multiple_of(mine0, LANES), HALF)].astype(F32)
    xf[c, :, pl.ds(HALF, LANES)] = pick
    pl.semaphore_wait(barrier, len(partners))
    swap = remote(xs, xf.at[c], x_sem.at[0], x_sem.at[1], sibling)
    swap.start()

    for i in (1, 2):
        for j in range(6):
            w_copy(i, j).start()
    for i in range(1, 8):
        m_copy(i).start()
    for i in (6, 7, 0, 1, 2):
        inward[i].wait()
    for e in range(3):
        for h in range(2):
            out_bd[pl.ds(e * 32 + h * 16, 16), pl.ds((h * 3 + e) * LANES, LANES)] = out_maps[e, h]
        a_bd[pl.ds(e * 16, 16), pl.ds(e * LANES, LANES)] = a_t[e]
    swap.wait_send()
    remote(xs, xf.at[o], x_sem.at[0], x_sem.at[1], sibling).wait_recv()
    block = xf[...].reshape(ROWS, HALF + LANES).astype(BF16)
    for u, (order, first, cols) in enumerate(UNITS):
        G[u][x, y, z, :, pl.ds(0, cols)] = block[:, first : first + cols]
        if u == PICK_UNIT:
            G[u][x, y, z, :, pl.ds(cols, LANES)] = block[:, HALF:]

    def ag(u, k, piece, kind, arriving=False):
        order = UNITS[u][0]
        if kind == 2:
            step = 1 if piece in ((0,) if k == 0 else (0, 1)) else -1
            q = -2 * step if arriving else -step
        else:
            step = 1 if kind == 0 else -1
            q = -step if arriving else 0
        which = None if k == 0 and kind < 2 else piece
        block = G[u].at[part(order, k, q, which, gathered_width(u))]
        sem = AG_GROUP_OF[(k, piece, kind)]
        return remote(block, block, ag_s.at[u, k], ag_r.at[u, sem], along(order[k], step))

    def ag_send(u, k, piece):
        ag(u, k, piece, 0).start()
        ag(u, k, piece, 1).start()

    def blocks_of(ref, k, n, cols):
        ix = [0, 0, 0, pl.ds(0, ROWS), pl.ds(0, cols)]
        if k > 0:
            ix[3 - k] = pl.ds(0, n)
            for j in range(4 - k, 3):
                ix[j] = pl.ds(0, SIDE)
        return ref.at[tuple(ix)]

    def ag_got(u, i):
        k, _, kind = AG_GROUPS[i][0]
        n = len(AG_GROUPS[i])
        if k == 0:
            n = 1
        ref = blocks_of(G[u], max(k, 1), n, gathered_width(u))
        remote(ref, ref, ag_s.at[u, k], ag_r.at[u, i], sibling).wait_recv()

    def ag_pass(u, k, piece):
        ag(u, k, piece, 2).start()

    def ag_left(u, k):
        ref = blocks_of(G[u], k + 1, 3, gathered_width(u))
        remote(ref, ref, ag_s.at[u, k], ag_r.at[u, 0], sibling).wait_send()

    def line_a(u):
        ag_got(u, 0)
        ag_pass(u, 0, 0)
        ag_send(u, 1, -1)
        ag_got(u, 1)
        ag_pass(u, 0, 1)
        ag_send(u, 1, 1)

    def line_b(u):
        ag_got(u, 2)
        ag_send(u, 1, 2)
        ag_send(u, 2, 0)

    def plane_a(u):
        ag_got(u, 3)
        ag_pass(u, 1, 0)
        ag_pass(u, 1, -1)
        ag_got(u, 4)
        ag_pass(u, 1, 1)
        ag_pass(u, 1, 2)

    def plane_b(u):
        ag_got(u, 5)
        ag_send(u, 2, -1)
        ag_got(u, 6)
        ag_send(u, 2, 1)

    def plane_c(u):
        ag_got(u, 7)
        ag_send(u, 2, 2)
        hand(u, None, 0).start()

    def cube_a(u, piece):
        ag_got(u, {0: 8, -1: 9, 1: 10, 2: 11}[piece])
        ag_pass(u, 2, piece)
        hand(u, piece, -1).start()
        hand(u, piece, 1).start()

    def cube_b(u, i):
        ag_got(u, 12 + i)
        for r, q in (FAR_A, FAR_B)[i]:
            hand(u, r, q).start()

    def hand(u, piece, q):
        order, _, cols = UNITS[u]
        block = part(order, 2, q, piece, cols)
        (i,) = (i for i, rows in enumerate(HAND_GROUPS) if (piece, q) in rows)
        return remote(G[u].at[block], O[u].at[block], as_s.at[u], as_r.at[u, i], sibling)

    def gate_up(u, src, first0, rows):
        order, first, cols = UNITS[u]
        ws = pl.ds(pl.multiple_of(first0 + first, LANES), cols)
        if len(rows) == 1:
            lhs = src[part(order, 2, rows[0][1], None, cols)].reshape(256, cols)
            at_a = part(order, 2, rows[0][1], None, GU)
            acc[at_a] = acc[at_a] + dot(lhs, gu[ws, :]).reshape(SIDE, SIDE, ROWS, GU)
            return
        lhs = jnp.concatenate([src[part(order, 2, q, r, cols)].reshape(64, cols) for r, q in rows], axis=0)
        got = dot(lhs, gu[ws, :])
        for i, (r, q) in enumerate(rows):
            at_a = part(order, 2, q, r, GU)
            acc[at_a] = acc[at_a] + got[i * 64 : (i + 1) * 64].reshape(SIDE, ROWS, GU)

    def from_sibling(u, rows):
        n = SIDE if rows is HERE else len(rows)
        ref = blocks_of(O[u], 2, n, UNITS[u][2])
        remote(ref, ref, as_s.at[u], as_r.at[u, HAND_GROUPS.index(rows)], sibling).wait_recv()
        gate_up(u, O[u], other0, rows)

    def shared(u, src, first0):
        _, first, cols = UNITS[u]
        ws = pl.ds(pl.multiple_of(first0 + first, LANES), cols)
        acc_s[...] += dot(src[x, pl.ds(2 * c, 2), :, :, pl.ds(0, cols)].reshape(128, cols), sgu[ws, :])

    def merge_up(first, n):
        def body(i, carry):
            kb = first + i * 4
            ab = dot_t(in_v[:, :, pl.ds(pl.multiple_of(kb * QB, QB), 4 * QB)].reshape(96, 4 * QB), out_bd[...])
            for t in range(4):
                ks = pl.ds(pl.multiple_of(kb * QB, QB) + t * QB, QB)
                for j in range(6):
                    cs = pl.ds(j * LANES, LANES)
                    s = (gate_s if j < 3 else up_s)[j % 3, 0, kb + t]
                    add = ab[t * QB : (t + 1) * QB, j * LANES : (j + 1) * LANES]
                    gu[ks, cs] = (gu[ks, cs].astype(F32) * s + add).astype(BF16)
            return carry

        lax.fori_loop(0, n, body, 0)

    def merge_down(first, n):
        def body(i, carry):
            n0 = pl.multiple_of((first + i) * 1024, 1024)
            ab = dot_t(a_bd[...], b_v[:, :, pl.ds(n0, 1024)].reshape(48, 1024))
            for e in range(3):
                for t in range(8):
                    at_d = (pl.ds(e * LANES, LANES), pl.ds(n0 + t * QB, QB))
                    s = down_s[e, 0, (first + i) * 8 + t]
                    add = ab[e * LANES : (e + 1) * LANES, t * QB : (t + 1) * QB]
                    dcat[at_d] = (dcat[at_d].astype(F32) * s + add).astype(BF16)
            return carry

        lax.fori_loop(0, n, body, 0)

    def wait_w(i):
        wait_all(gu.at[pl.ds(*w_rows[i])], w_sem.at[i])

    ALL = range(NU)
    for u in ALL:
        ag_send(u, 0, 0)
    for u in ALL:
        ag_send(u, 1, 0)
    acc[...] = jnp.zeros_like(acc)
    acc_s[...] = jnp.zeros_like(acc_s)
    m_copy(0).wait()
    wait_w(0)
    merge_up(c * 28, 2)
    for u in ALL:
        line_a(u)
    merge_up(c * 28 + 8, 1)
    wait_w(1)
    merge_up(c * 28 + 12, 2)
    for u in ALL:
        line_b(u)
    merge_up(c * 28 + 20, 2)
    for u in ALL:
        plane_a(u)
    wait_w(2)
    merge_up(o * 28, 2)
    for u in ALL:
        plane_b(u)
    merge_up(o * 28 + 8, 2)
    for u in ALL:
        plane_c(u)
    merge_up(o * 28 + 16, 3)
    for u in ALL:
        gate_up(u, G[u], mine0, HERE)
    for u in ALL:
        cube_a(u, 0)
    for u in ALL:
        from_sibling(u, HERE)
    m_copy(3).wait()
    wait_all(dcat, m_sem.at[3])
    merge_down(0, 3)
    for u in ALL:
        cube_a(u, -1)
    for u in ALL:
        gate_up(u, G[u], mine0, NEAR_A)
    merge_down(3, 4)
    for u in ALL:
        cube_a(u, 1)
    for u in ALL:
        from_sibling(u, NEAR_A)
    for u in ALL:
        cube_a(u, 2)
    for u in ALL:
        gate_up(u, G[u], mine0, NEAR_B)
    for u in ALL:
        from_sibling(u, NEAR_B)
    wait_all(sgu, m_sem.at[1])
    for u in ALL:
        cube_b(u, 0)
    for u in ALL:
        gate_up(u, G[u], mine0, FAR_A)
    for u in ALL:
        from_sibling(u, FAR_A)
    for u in ALL:
        for k in (0, 1):
            ag_left(u, k)
    for u in ALL:
        cube_b(u, 1)
    for u in ALL:
        gate_up(u, G[u], mine0, FAR_B)
        shared(u, G[u], mine0)
    for u in ALL:
        from_sibling(u, FAR_B)
        shared(u, O[u], other0)

    choose = (
        lax.broadcasted_iota(jnp.int32, (LANES, HID), 0)
        == lax.broadcasted_iota(jnp.int32, (LANES, HID), 1) // LANES + g * 3
    ).astype(BF16)
    pick_cols = pl.ds(UNITS[PICK_UNIT][2], LANES)

    def silu(v):
        return 0.5 * v * (1.0 + jnp.tanh(0.5 * v))

    def activate(i, carry):
        gate = acc[i, :, :, :, pl.ds(0, HID)].reshape(256, HID)
        up = acc[i, :, :, :, pl.ds(HID, HID)].reshape(256, HID)
        picks = dot(G[PICK_UNIT][i, :, :, :, pick_cols].reshape(256, LANES), choose)
        hcat[i, :, :, :, pl.ds(0, HID)] = (silu(gate) * up * picks).astype(BF16).reshape(SIDE, SIDE, ROWS, HID)
        return carry

    lax.fori_loop(0, SIDE, activate, 0)
    sg = acc_s[:, pl.ds(0, LANES)]
    su = acc_s[:, pl.ds(LANES, LANES)]
    hcat[x, pl.ds(2 * c, 2), :, :, pl.ds(HID, LANES)] = (
        (silu(sg) * su).astype(BF16).reshape(2, SIDE, ROWS, LANES)
    )

    def rows_of(u, q):
        return hcat[part(UNITS[u][0], 2, q, None, DOWN)].reshape(256, DOWN)

    def give(u, q):
        order, _, cols = UNITS[u]
        block = part(order, 2, q, None, cols)
        return remote(O[u].at[block], S[u].at[block], ss_s.at[u], ss_r.at[u, REL.index(q)], sibling)

    def down_other(u, q):
        order, first, cols = UNITS[u]
        ns = pl.ds(pl.multiple_of(other0 + first, LANES), cols)
        theirs = dot(rows_of(u, q), dcat[:, ns]).astype(BF16)
        O[u][part(order, 2, q, None, cols)] = theirs.reshape(SIDE, SIDE, ROWS, cols)
        give(u, q).start()

    def down_mine(u, q):
        order, first, cols = UNITS[u]
        block = part(order, 2, q, None, cols)
        ns = pl.ds(pl.multiple_of(mine0 + first, LANES), cols)
        mine = dot(rows_of(u, q), dcat[:, ns]).reshape(SIDE, SIDE, ROWS, cols)
        give(u, q).wait_recv()
        G[u][block] = (mine + S[u][block].astype(F32)).astype(BF16)

    def rs_part(k, q, piece, h, order, cols):
        ix = part(order, k, q, piece if k else None, cols)
        return (*ix[:4], halved(cols, h))

    def rs_land(slot, k, piece, h, order, cols):
        ix = landing(slot, order, k, piece if k else None, at, cols)
        return (*ix[:-1], halved(cols, h))

    def rs_sem(k, piece, kind):
        return (16 if k == 0 else (2 - k) * 8 + REL.index(piece) * 2) + min(kind, 1)

    def rs(u, k, piece, kind, step):
        order, _, cols = UNITS[u]
        h = 0 if (step == 1) == (kind != 1) else 1
        slot = 0 if kind == 0 else (1 if step == 1 else 2)
        src = G[u].at[rs_part(k, 2 if kind == 0 else step, piece, h, order, cols)]
        dst = R[u][k].at[rs_land(slot, k, piece, h, order, cols)]
        return remote(src, dst, rs_s.at[u, k], rs_r.at[u, rs_sem(k, piece, kind)], along(order[k], step))

    def rs_far(u, k, piece):
        rs(u, k, piece, 0, 1).start()
        rs(u, k, piece, 0, -1).start()

    def rs_near(u, k, piece, step):
        rs(u, k, piece, 1, step).start()

    def rs_got(u, k, piece, kind):
        ref = blocks_of(G[u], max(k, 1), 2 if kind else 1, UNITS[u][2])
        remote(ref, ref, rs_s.at[u, k], rs_r.at[u, rs_sem(k, piece, kind)], sibling).wait_recv()

    def rs_pass(u, k, piece):
        order, _, cols = UNITS[u]
        rs_got(u, k, piece, 0)
        for h, step in ((0, 1), (1, -1)):
            block = rs_part(k, step, piece, h, order, cols)
            came = R[u][k][rs_land(0, k, piece, h, order, cols)]
            G[u][block] = (G[u][block].astype(F32) + came.astype(F32)).astype(BF16)
            rs(u, k, piece, 2, step).start()

    def rs_sum(u, k, piece):
        order, _, cols = UNITS[u]
        rs_got(u, k, piece, 1)
        block = rs_part(k, 0, piece, None, order, cols)
        l = R[u][k][rs_land(1, k, piece, None, order, cols)]
        r = R[u][k][rs_land(2, k, piece, None, order, cols)]
        total = G[u][block].astype(F32) + (l.astype(F32) + r.astype(F32))
        if k > 0:
            G[u][block] = total.astype(BF16)
            for p in (2, 1, -1, 0) if k == 2 else (0,):
                if piece == 2:
                    rs_far(u, k - 1, p)
                elif piece != 0:
                    rs_near(u, k - 1, p, piece)
        return total

    for u in ALL:
        ag_left(u, 2)
        ref = G[u].at[:, :, :, :, pl.ds(0, UNITS[u][2])]
        remote(ref, ref, as_s.at[u], as_r.at[u, 0], sibling).wait_send()
    for u in ALL:
        down_other(u, 2)
    for u in ALL:
        down_other(u, 1)
    for u in ALL:
        down_mine(u, 2)
        rs_far(u, 2, 2)
        rs_far(u, 2, 1)
    for u in ALL:
        down_other(u, -1)
    for u in ALL:
        down_mine(u, 1)
        rs_near(u, 2, 2, 1)
    for u in ALL:
        down_mine(u, -1)
        rs_near(u, 2, 2, -1)
        rs_far(u, 2, -1)
    for u in ALL:
        rs_near(u, 2, 1, 1)
        rs_near(u, 2, 1, -1)
        rs_far(u, 2, 0)
    for u in ALL:
        rs_pass(u, 2, 2)
    for u in ALL:
        rs_near(u, 2, -1, 1)
        rs_near(u, 2, -1, -1)
    for u in ALL:
        down_other(u, 0)
    for u in ALL:
        rs_pass(u, 2, 1)
    for u in ALL:
        rs_near(u, 2, 0, 1)
        rs_near(u, 2, 0, -1)
    for u in ALL:
        down_mine(u, 0)
    for u in ALL:
        rs_sum(u, 2, 2)
    for u in ALL:
        rs_pass(u, 2, -1)
    for u in ALL:
        rs_sum(u, 2, 1)
    for u in ALL:
        rs_pass(u, 2, 0)
    for u in ALL:
        rs_sum(u, 2, -1)
    for p in (2, 1, -1, 0):
        for u in ALL:
            rs_pass(u, 1, p)
    for u in ALL:
        rs_sum(u, 2, 0)
    for p in (2, 1, -1):
        for u in ALL:
            rs_sum(u, 1, p)
    for u in ALL:
        rs_pass(u, 0, 0)
    for u in ALL:
        rs_sum(u, 1, 0)
    for u in ALL:
        _, first, cols = UNITS[u]
        fs[:, :, pl.ds(first, cols)] = rs_sum(u, 0, 0).reshape(2, 8, cols)

    final = remote(fs.at[o], fr, x_sem.at[2], x_sem.at[3], sibling)
    final.start()
    out[:, pl.ds(pl.multiple_of(mine0, LANES), HALF)] = fs[c].astype(BF16)
    final.wait_recv()
    out[:, pl.ds(pl.multiple_of(other0, LANES), HALF)] = fr[...].astype(BF16)
    final.wait_send()
    for u in ALL:
        for k in range(3):
            ref = blocks_of(G[u], k + 1, 3, UNITS[u][2])
            remote(ref, ref, rs_s.at[u, k], rs_r.at[u, 0], sibling).wait_send()
        remote(O[u], O[u], ss_s.at[u], ss_r.at[u, 0], sibling).wait_send()


def on_device(
    tokens,
    picked_group_index,
    picked_expert_index,
    routing_pick_weight,
    common_gate_weight,
    common_up_weight,
    common_down_weight,
    routed_gate_weight,
    routed_up_weight,
    routed_down_weight,
    gate_block_scales,
    up_block_scales,
    down_block_scales,
    adapter_input_maps,
    adapter_output_maps,
    adapter_down_input,
    adapter_down_output,
):
    vmem = pl.BlockSpec(memory_space=pltpu.VMEM)
    hbm = pl.BlockSpec(memory_space=pl.ANY)
    scratch = []
    for u in range(NU):
        scratch.append(pltpu.VMEM((SIDE, SIDE, SIDE, ROWS, gathered_width(u)), BF16))
    for _ in range(2):
        for _, _, cols in UNITS:
            scratch.append(pltpu.VMEM((SIDE, SIDE, SIDE, ROWS, cols), BF16))
    for _, _, cols in UNITS:
        for k in range(3):
            scratch.append(pltpu.VMEM((3, *([SIDE] * k), ROWS, cols), BF16))
    scratch += [
        pltpu.VMEM((WIDTH, GU), BF16),
        pltpu.VMEM((WIDTH, 2 * LANES), BF16),
        pltpu.VMEM((DOWN, WIDTH), BF16),
        pltpu.VMEM((3, 32, WIDTH), BF16),
        pltpu.VMEM((3, 16, WIDTH), BF16),
        pltpu.VMEM((SIDE, SIDE, SIDE, ROWS, GU), F32),
        pltpu.VMEM((128, 2 * LANES), F32),
        pltpu.VMEM((SIDE, SIDE, SIDE, ROWS, DOWN), BF16),
        pltpu.VMEM((96, GU), BF16),
        pltpu.VMEM((48, HID), BF16),
        pltpu.VMEM((8, HALF + LANES), F32),
        pltpu.VMEM((2, 8, HALF + LANES), F32),
        pltpu.VMEM((2, 8, HALF), F32),
        pltpu.VMEM((8, HALF), F32),
        pltpu.SMEM((3, 1, WIDTH // QB), F32),
        pltpu.SMEM((3, 1, WIDTH // QB), F32),
        pltpu.SMEM((3, 1, WIDTH // QB), F32),
        pltpu.VMEM((8, WIDTH), BF16),
        pltpu.VMEM((8, 8), jnp.int32),
        pltpu.VMEM((8, 8), BF16),
        pltpu.VMEM((3, 2, 16, LANES), BF16),
        pltpu.VMEM((3, 16, LANES), BF16),
        pltpu.SemaphoreType.DMA((8,)),
        pltpu.SemaphoreType.DMA((3,)),
        pltpu.SemaphoreType.DMA((4,)),
        pltpu.SemaphoreType.DMA((4,)),
        pltpu.SemaphoreType.DMA((NU, 3)),
        pltpu.SemaphoreType.DMA((NU, AG_WAITS)),
        pltpu.SemaphoreType.DMA((NU,)),
        pltpu.SemaphoreType.DMA((NU, 5)),
        pltpu.SemaphoreType.DMA((NU, 3)),
        pltpu.SemaphoreType.DMA((NU, 18)),
        pltpu.SemaphoreType.DMA((NU,)),
        pltpu.SemaphoreType.DMA((NU, 4)),
    ]
    return pl.pallas_call(
        kernel,
        out_shape=jax.ShapeDtypeStruct((8, WIDTH), BF16),
        in_specs=[hbm] * 16,
        out_specs=vmem,
        scratch_shapes=scratch,
        compiler_params=pltpu.CompilerParams(
            collective_id=0, has_side_effects=True, vmem_limit_bytes=62 * 2**20
        ),
        cost_estimate=pl.CostEstimate(flops=22 * 10**9, bytes_accessed=25 * 10**6, transcendentals=10**6),
    )(
        gate_block_scales.transpose(0, 2, 1),
        up_block_scales.transpose(0, 2, 1),
        down_block_scales,
        tokens,
        picked_expert_index,
        routing_pick_weight,
        adapter_output_maps,
        adapter_down_input.transpose(0, 2, 1),
        routed_gate_weight,
        routed_up_weight,
        routed_down_weight,
        common_gate_weight,
        common_up_weight,
        common_down_weight,
        adapter_input_maps.transpose(0, 2, 1),
        adapter_down_output,
    )


def solution(mesh):
    in_specs = (
        P(("group", "local"), None),
        P(("group", "local"), None),
        P(("group", "local"), None),
        P(("group", "local"), None),
        P(None, "local"),
        P(None, "local"),
        P("local", None),
        P("group", None, "local"),
        P("group", None, "local"),
        P("group", "local", None),
        P("group", None, "local"),
        P("group", None, "local"),
        P("group", "local", None),
        P("group", None, None),
        P("group", None, None, "local"),
        P("group", "local", None),
        P("group", None, None),
    )
    return jax.shard_map(
        on_device, mesh=mesh, in_specs=in_specs, out_specs=P(("group", "local"), None), check_vma=False
    )
```

time: 117 us -> 100 us (0.85)
  Pallas kernels: 112 us -> 98.4 us
  other arithmetic: 2.76 us -> 0 us
    pallas_call x1, Pallas kernels: 112 us -> 98.4 us  [on_device(): pl.pallas_call(kernel, out_shape=jax.ShapeDtypeStruct((8, WIDTH), BF16),...]
    unnamed x3 -> x0, other arithmetic: 2.1 us -> none
where the time goes in v2:
time: 100 us
  Pallas kernels  98.4 us (98%)
  local copies, waits for them, and re-layouts  1.55 us (2%)
    pallas_call x1, Pallas kernels, on_device(): pl.pallas_call(kernel, out_shape=jax.ShapeDtypeStruct((8, WIDTH), BF16),...  98.4 us

profile of v2, /device:TPU:1, one launch (start us, length us, event | category | flops | bytes accessed | tf_op | source)
XLA Modules:
  0.0 100.0 jit_solution(2022940102909150581)
XLA Ops:
  0.0 98.4 %shard_map.154 = bf16[8,7168]{1,0:T(8,128)(2,1)} custom-call(f32[3,1,56]{2,1,0:T(1,128)} %bitcast.6, f32[3,1,56]{2,1,0:T(1,128)} %bitcast.7, f32[3,1,56]{2,1,0:T(1,128)} %refs_2_.1, bf16[8,7168]{1,0:T(8,128)(2,1)} %refs_3_.1, s32[8,8]{1,0:T(8,128)} %refs_4_.1, bf16[8,8]{1,0:T(8,128)(2,1)} %refs_5_.1, bf16[3,2,16,128]{3,2,1,0:T(8,128)(2,1)} %refs_6_.1, ...), custom_call_target="tpu_custom_call" | custom-call | flops 22000001024 | bytes 25000000 | tf_op jit(solution)/shard_map/pallas_call | solution.py:676
  98.4 1.6 %copy.18 = bf16[8,7168]{1,0:T(8,128)(2,1)} copy(bf16[8,7168]{1,0:T(8,128)(2,1)} %shard_map.154) | data formatting | bytes 229376

commit v3 on v2

--- a/solution.py
+++ b/solution.py
@@ -51,9 +51,17 @@
 HERE = ((None, 0),)
 NEAR_A = ((0, -1), (0, 1), (-1, -1), (-1, 1))
 NEAR_B = ((1, -1), (1, 1), (2, -1), (2, 1))
-FAR_A = ((0, 2), (-1, 2))
-FAR_B = ((1, 2), (2, 2))
-HAND_GROUPS = (HERE, NEAR_A, NEAR_B, FAR_A, FAR_B)
+FAR = ((0, 2), (-1, 2), (1, 2), (2, 2))
+HAND_GROUPS = (HERE, NEAR_A, NEAR_B, FAR)
+GIVE_GROUPS = (
+    ((2, 2),),
+    ((1, 2),),
+    ((2, 1), (2, -1)),
+    ((-1, 2), (1, 1), (1, -1)),
+    ((0, 2), (-1, 1), (-1, -1)),
+    ((0, 1), (0, -1)),
+    ((2, 0), (1, 0), (-1, 0), (0, 0)),
+)
 
 
 def gathered_width(u):
@@ -251,6 +259,15 @@
         ref = blocks_of(G[u], k + 1, 3, gathered_width(u))
         remote(ref, ref, ag_s.at[u, k], ag_r.at[u, 0], sibling).wait_send()
 
+    def ag_block(u, j):
+        order = UNITS[u][0]
+        ix = list(part(order, 2, 0, 0, gathered_width(u)))
+        ix[order[0]] = at(order[0], j)
+        block = G[u].at[tuple(ix)]
+        for kind, step in ((0, 1), (1, -1)):
+            sem = AG_GROUP_OF[(2, 0, kind)]
+            remote(block, block, ag_s.at[u, 2], ag_r.at[u, sem], along(order[2], step)).start()
+
     def line_a(u):
         ag_got(u, 0)
         ag_pass(u, 0, 0)
@@ -262,7 +279,7 @@
     def line_b(u):
         ag_got(u, 2)
         ag_send(u, 1, 2)
-        ag_send(u, 2, 0)
+        ag_block(u, 2)
 
     def plane_a(u):
         ag_got(u, 3)
@@ -291,7 +308,7 @@
 
     def cube_b(u, i):
         ag_got(u, 12 + i)
-        for r, q in (FAR_A, FAR_B)[i]:
+        for r, q in FAR[2 * i : 2 * i + 2]:
             hand(u, r, q).start()
 
     def hand(u, piece, q):
@@ -302,6 +319,8 @@
 
     def gate_up(u, src, first0, rows):
         order, first, cols = UNITS[u]
+        if rows is FAR:
+            rows = ((None, 2),)
         ws = pl.ds(pl.multiple_of(first0 + first, LANES), cols)
         if len(rows) == 1:
             lhs = src[part(order, 2, rows[0][1], None, cols)].reshape(256, cols)
@@ -362,6 +381,8 @@
         ag_send(u, 0, 0)
     for u in ALL:
         ag_send(u, 1, 0)
+    for u in ALL:
+        ag_block(u, 0)
     acc[...] = jnp.zeros_like(acc)
     acc_s[...] = jnp.zeros_like(acc_s)
     m_copy(0).wait()
@@ -369,36 +390,39 @@
     merge_up(c * 28, 2)
     for u in ALL:
         line_a(u)
+    for u in ALL:
+        ag_block(u, -1)
+        ag_block(u, 1)
     merge_up(c * 28 + 8, 1)
     wait_w(1)
     merge_up(c * 28 + 12, 2)
     for u in ALL:
         line_b(u)
     merge_up(c * 28 + 20, 2)
+    wait_w(2)
+    merge_up(o * 28, 1)
     for u in ALL:
         plane_a(u)
-    wait_w(2)
-    merge_up(o * 28, 2)
+    merge_up(o * 28 + 4, 3)
     for u in ALL:
         plane_b(u)
-    merge_up(o * 28 + 8, 2)
-    for u in ALL:
-        plane_c(u)
     merge_up(o * 28 + 16, 3)
-    for u in ALL:
-        gate_up(u, G[u], mine0, HERE)
-    for u in ALL:
-        cube_a(u, 0)
-    for u in ALL:
-        from_sibling(u, HERE)
     m_copy(3).wait()
     wait_all(dcat, m_sem.at[3])
-    merge_down(0, 3)
+    merge_down(0, 2)
+    for u in ALL:
+        plane_c(u)
+    for u in ALL:
+        gate_up(u, G[u], mine0, HERE)
+    for u in ALL:
+        cube_a(u, 0)
+    for u in ALL:
+        from_sibling(u, HERE)
     for u in ALL:
         cube_a(u, -1)
+    merge_down(2, 2)
     for u in ALL:
         gate_up(u, G[u], mine0, NEAR_A)
-    merge_down(3, 4)
     for u in ALL:
         cube_a(u, 1)
     for u in ALL:
@@ -407,25 +431,23 @@
         cube_a(u, 2)
     for u in ALL:
         gate_up(u, G[u], mine0, NEAR_B)
+    merge_down(4, 3)
     for u in ALL:
         from_sibling(u, NEAR_B)
     wait_all(sgu, m_sem.at[1])
     for u in ALL:
         cube_b(u, 0)
     for u in ALL:
-        gate_up(u, G[u], mine0, FAR_A)
-    for u in ALL:
-        from_sibling(u, FAR_A)
-    for u in ALL:
         for k in (0, 1):
             ag_left(u, k)
     for u in ALL:
         cube_b(u, 1)
     for u in ALL:
-        gate_up(u, G[u], mine0, FAR_B)
+        gate_up(u, G[u], mine0, FAR)
+    for u in ALL:
         shared(u, G[u], mine0)
     for u in ALL:
-        from_sibling(u, FAR_B)
+        from_sibling(u, FAR)
         shared(u, O[u], other0)
 
     choose = (
@@ -454,25 +476,31 @@
     def rows_of(u, q):
         return hcat[part(UNITS[u][0], 2, q, None, DOWN)].reshape(256, DOWN)
 
-    def give(u, q):
+    def give(u, r, q):
         order, _, cols = UNITS[u]
-        block = part(order, 2, q, None, cols)
-        return remote(O[u].at[block], S[u].at[block], ss_s.at[u], ss_r.at[u, REL.index(q)], sibling)
+        block = part(order, 2, q, r, cols)
+        (i,) = (i for i, rows in enumerate(GIVE_GROUPS) if (r, q) in rows)
+        return remote(O[u].at[block], S[u].at[block], ss_s.at[u], ss_r.at[u, i], sibling)
 
     def down_other(u, q):
         order, first, cols = UNITS[u]
         ns = pl.ds(pl.multiple_of(other0 + first, LANES), cols)
         theirs = dot(rows_of(u, q), dcat[:, ns]).astype(BF16)
         O[u][part(order, 2, q, None, cols)] = theirs.reshape(SIDE, SIDE, ROWS, cols)
-        give(u, q).start()
 
     def down_mine(u, q):
         order, first, cols = UNITS[u]
-        block = part(order, 2, q, None, cols)
         ns = pl.ds(pl.multiple_of(mine0 + first, LANES), cols)
-        mine = dot(rows_of(u, q), dcat[:, ns]).reshape(SIDE, SIDE, ROWS, cols)
-        give(u, q).wait_recv()
-        G[u][block] = (mine + S[u][block].astype(F32)).astype(BF16)
+        mine = dot(rows_of(u, q), dcat[:, ns]).astype(BF16)
+        G[u][part(order, 2, q, None, cols)] = mine.reshape(SIDE, SIDE, ROWS, cols)
+
+    def take_in(u, i):
+        order, _, cols = UNITS[u]
+        ref = blocks_of(S[u], 2, len(GIVE_GROUPS[i]), cols)
+        remote(ref, ref, ss_s.at[u], ss_r.at[u, i], sibling).wait_recv()
+        for r, q in GIVE_GROUPS[i]:
+            block = part(order, 2, q, r, cols)
+            G[u][block] = (G[u][block].astype(F32) + S[u][block].astype(F32)).astype(BF16)
 
     def rs_part(k, q, piece, h, order, cols):
         ix = part(order, k, q, piece if k else None, cols)
@@ -530,48 +558,65 @@
         return total
 
     for u in ALL:
+        down_other(u, 2)
+        give(u, 2, 2).start()
+        give(u, 1, 2).start()
+    for u in ALL:
         ag_left(u, 2)
         ref = G[u].at[:, :, :, :, pl.ds(0, UNITS[u][2])]
         remote(ref, ref, as_s.at[u], as_r.at[u, 0], sibling).wait_send()
     for u in ALL:
-        down_other(u, 2)
-    for u in ALL:
-        down_other(u, 1)
-    for u in ALL:
         down_mine(u, 2)
+        take_in(u, 0)
         rs_far(u, 2, 2)
+    for q in (1, -1):
+        for u in ALL:
+            down_other(u, q)
+            give(u, 2, q).start()
+    for u in ALL:
+        take_in(u, 1)
         rs_far(u, 2, 1)
     for u in ALL:
-        down_other(u, -1)
+        for r, q in GIVE_GROUPS[3]:
+            give(u, r, q).start()
     for u in ALL:
         down_mine(u, 1)
+        down_mine(u, -1)
+        take_in(u, 2)
         rs_near(u, 2, 2, 1)
-    for u in ALL:
-        down_mine(u, -1)
         rs_near(u, 2, 2, -1)
+    for u in ALL:
+        for r, q in GIVE_GROUPS[4]:
+            give(u, r, q).start()
+    for u in ALL:
+        rs_pass(u, 2, 2)
+        take_in(u, 3)
         rs_far(u, 2, -1)
-    for u in ALL:
         rs_near(u, 2, 1, 1)
         rs_near(u, 2, 1, -1)
+    for u in ALL:
+        for r, q in GIVE_GROUPS[5]:
+            give(u, r, q).start()
+    for u in ALL:
+        down_other(u, 0)
+        for r, q in GIVE_GROUPS[6]:
+            give(u, r, q).start()
+    for u in ALL:
+        rs_pass(u, 2, 1)
+        take_in(u, 4)
         rs_far(u, 2, 0)
-    for u in ALL:
-        rs_pass(u, 2, 2)
-    for u in ALL:
         rs_near(u, 2, -1, 1)
         rs_near(u, 2, -1, -1)
     for u in ALL:
-        down_other(u, 0)
-    for u in ALL:
-        rs_pass(u, 2, 1)
-    for u in ALL:
+        down_mine(u, 0)
+        take_in(u, 6)
+    for u in ALL:
+        rs_sum(u, 2, 2)
+    for u in ALL:
+        rs_pass(u, 2, -1)
+        take_in(u, 5)
         rs_near(u, 2, 0, 1)
         rs_near(u, 2, 0, -1)
-    for u in ALL:
-        down_mine(u, 0)
-    for u in ALL:
-        rs_sum(u, 2, 2)
-    for u in ALL:
-        rs_pass(u, 2, -1)
     for u in ALL:
         rs_sum(u, 2, 1)
     for u in ALL:
@@ -667,11 +712,11 @@
         pltpu.SemaphoreType.DMA((NU, 3)),
         pltpu.SemaphoreType.DMA((NU, AG_WAITS)),
         pltpu.SemaphoreType.DMA((NU,)),
-        pltpu.SemaphoreType.DMA((NU, 5)),
+        pltpu.SemaphoreType.DMA((NU, 4)),
         pltpu.SemaphoreType.DMA((NU, 3)),
         pltpu.SemaphoreType.DMA((NU, 18)),
         pltpu.SemaphoreType.DMA((NU,)),
-        pltpu.SemaphoreType.DMA((NU, 4)),
+        pltpu.SemaphoreType.DMA((NU, 7)),
     ]
     return pl.pallas_call(
         kernel,

time: 100 us -> 93.7 us (0.937)
  Pallas kernels: 98.4 us -> 92 us
    pallas_call x1, Pallas kernels: 98.4 us -> 92 us  [on_device(): pl.pallas_call(kernel, out_shape=jax.ShapeDtypeStruct((8, WIDTH), BF16),...]
where the time goes in v3:
time: 93.7 us; the launch traced here: 93.6 us
  Pallas kernels  92 us (98%)
  local copies, waits for them, and re-layouts  1.55 us (2%)
    pallas_call x1, Pallas kernels, on_device(): pl.pallas_call(kernel, out_shape=jax.ShapeDtypeStruct((8, WIDTH), BF16),...  92 us

profile of v3, /device:TPU:1, one launch (start us, length us, event | category | flops | bytes accessed | tf_op | source)
XLA Modules:
  0.0 93.6 jit_solution(9429966074223097313)
XLA Ops:
  0.0 92.0 %shard_map.154 = bf16[8,7168]{1,0:T(8,128)(2,1)} custom-call(f32[3,1,56]{2,1,0:T(1,128)} %bitcast.6, f32[3,1,56]{2,1,0:T(1,128)} %bitcast.7, f32[3,1,56]{2,1,0:T(1,128)} %refs_2_.1, bf16[8,7168]{1,0:T(8,128)(2,1)} %refs_3_.1, s32[8,8]{1,0:T(8,128)} %refs_4_.1, bf16[8,8]{1,0:T(8,128)(2,1)} %refs_5_.1, bf16[3,2,16,128]{3,2,1,0:T(8,128)(2,1)} %refs_6_.1, ...), custom_call_target="tpu_custom_call" | custom-call | flops 22000001024 | bytes 25000000 | tf_op jit(solution)/shard_map/pallas_call | solution.py:721
  92.1 1.6 %copy.18 = bf16[8,7168]{1,0:T(8,128)(2,1)} copy(bf16[8,7168]{1,0:T(8,128)(2,1)} %shard_map.154) | data formatting | bytes 229376

commit v4 on v3

--- a/solution.py
+++ b/solution.py
@@ -56,8 +56,9 @@
 GIVE_GROUPS = (
     ((2, 2),),
     ((1, 2),),
+    ((-1, 2),),
     ((2, 1), (2, -1)),
-    ((-1, 2), (1, 1), (1, -1)),
+    ((1, 1), (1, -1)),
     ((0, 2), (-1, 1), (-1, -1)),
     ((0, 1), (0, -1)),
     ((2, 0), (1, 0), (-1, 0), (0, 0)),
@@ -148,7 +149,7 @@
         )
 
     barrier = pltpu.get_barrier_semaphore()
-    partners = [along(a, s) for a in range(3) for s in (1, -1)] + [sibling]
+    partners = [along(a, s) for a in range(3) for s in (1, -1, 2)] + [sibling]
     for p in partners:
         pl.semaphore_signal(barrier, inc=1, device_id=p, device_id_type=MESH)
 
@@ -500,7 +501,7 @@
         remote(ref, ref, ss_s.at[u], ss_r.at[u, i], sibling).wait_recv()
         for r, q in GIVE_GROUPS[i]:
             block = part(order, 2, q, r, cols)
-            G[u][block] = (G[u][block].astype(F32) + S[u][block].astype(F32)).astype(BF16)
+            G[u][block] = G[u][block] + S[u][block]
 
     def rs_part(k, q, piece, h, order, cols):
         ix = part(order, k, q, piece if k else None, cols)
@@ -511,7 +512,7 @@
         return (*ix[:-1], halved(cols, h))
 
     def rs_sem(k, piece, kind):
-        return (16 if k == 0 else (2 - k) * 8 + REL.index(piece) * 2) + min(kind, 1)
+        return (2 - k) * 8 + REL.index(piece) * 2 + min(kind, 1)
 
     def rs(u, k, piece, kind, step):
         order, _, cols = UNITS[u]
@@ -538,8 +539,21 @@
         for h, step in ((0, 1), (1, -1)):
             block = rs_part(k, step, piece, h, order, cols)
             came = R[u][k][rs_land(0, k, piece, h, order, cols)]
-            G[u][block] = (G[u][block].astype(F32) + came.astype(F32)).astype(BF16)
+            G[u][block] = G[u][block] + came
             rs(u, k, piece, 2, step).start()
+
+    def rs_last(u, step):
+        order, _, cols = UNITS[u]
+        src = G[u].at[part(order, 0, step, None, cols)]
+        dst = R[u][0].at[landing({2: 0, 1: 1, -1: 2}[step], order, 0, None, at, cols)]
+        remote(src, dst, rs_s.at[u, 0], rs_r.at[u, 16], along(order[0], step)).start()
+
+    def rs_end(u):
+        order, _, cols = UNITS[u]
+        ref = blocks_of(G[u], 1, 3, cols)
+        remote(ref, ref, rs_s.at[u, 0], rs_r.at[u, 16], sibling).wait_recv()
+        f, l, r = (R[u][0][landing(i, order, 0, None, at, cols)].astype(F32) for i in range(3))
+        return G[u][part(order, 0, 0, None, cols)].astype(F32) + f + (l + r)
 
     def rs_sum(u, k, piece):
         order, _, cols = UNITS[u]
@@ -547,15 +561,15 @@
         block = rs_part(k, 0, piece, None, order, cols)
         l = R[u][k][rs_land(1, k, piece, None, order, cols)]
         r = R[u][k][rs_land(2, k, piece, None, order, cols)]
-        total = G[u][block].astype(F32) + (l.astype(F32) + r.astype(F32))
-        if k > 0:
-            G[u][block] = total.astype(BF16)
-            for p in (2, 1, -1, 0) if k == 2 else (0,):
+        G[u][block] = (G[u][block].astype(F32) + (l.astype(F32) + r.astype(F32))).astype(BF16)
+        if k == 1 and piece != 0:
+            rs_last(u, piece)
+        elif k == 2:
+            for p in (2, 1, -1, 0):
                 if piece == 2:
-                    rs_far(u, k - 1, p)
+                    rs_far(u, 1, p)
                 elif piece != 0:
-                    rs_near(u, k - 1, p, piece)
-        return total
+                    rs_near(u, 1, p, piece)
 
     for u in ALL:
         down_other(u, 2)
@@ -569,52 +583,54 @@
         down_mine(u, 2)
         take_in(u, 0)
         rs_far(u, 2, 2)
+        take_in(u, 1)
+        rs_far(u, 2, 1)
+    for u in ALL:
+        give(u, -1, 2).start()
+        give(u, 0, 2).start()
     for q in (1, -1):
         for u in ALL:
             down_other(u, q)
             give(u, 2, q).start()
-    for u in ALL:
-        take_in(u, 1)
-        rs_far(u, 2, 1)
-    for u in ALL:
-        for r, q in GIVE_GROUPS[3]:
-            give(u, r, q).start()
+            give(u, 1, q).start()
+    for u in ALL:
+        take_in(u, 2)
+        rs_far(u, 2, -1)
     for u in ALL:
         down_mine(u, 1)
         down_mine(u, -1)
-        take_in(u, 2)
+        take_in(u, 3)
         rs_near(u, 2, 2, 1)
         rs_near(u, 2, 2, -1)
     for u in ALL:
-        for r, q in GIVE_GROUPS[4]:
+        for r, q in GIVE_GROUPS[5][1:]:
             give(u, r, q).start()
     for u in ALL:
         rs_pass(u, 2, 2)
-        take_in(u, 3)
-        rs_far(u, 2, -1)
+        take_in(u, 4)
         rs_near(u, 2, 1, 1)
         rs_near(u, 2, 1, -1)
     for u in ALL:
-        for r, q in GIVE_GROUPS[5]:
-            give(u, r, q).start()
-    for u in ALL:
-        down_other(u, 0)
         for r, q in GIVE_GROUPS[6]:
             give(u, r, q).start()
     for u in ALL:
+        down_other(u, 0)
+        for r, q in GIVE_GROUPS[7]:
+            give(u, r, q).start()
+    for u in ALL:
         rs_pass(u, 2, 1)
-        take_in(u, 4)
+        take_in(u, 5)
         rs_far(u, 2, 0)
         rs_near(u, 2, -1, 1)
         rs_near(u, 2, -1, -1)
     for u in ALL:
         down_mine(u, 0)
+        take_in(u, 7)
+    for u in ALL:
+        rs_sum(u, 2, 2)
+    for u in ALL:
+        rs_pass(u, 2, -1)
         take_in(u, 6)
-    for u in ALL:
-        rs_sum(u, 2, 2)
-    for u in ALL:
-        rs_pass(u, 2, -1)
-        take_in(u, 5)
         rs_near(u, 2, 0, 1)
         rs_near(u, 2, 0, -1)
     for u in ALL:
@@ -632,12 +648,10 @@
         for u in ALL:
             rs_sum(u, 1, p)
     for u in ALL:
-        rs_pass(u, 0, 0)
-    for u in ALL:
         rs_sum(u, 1, 0)
     for u in ALL:
         _, first, cols = UNITS[u]
-        fs[:, :, pl.ds(first, cols)] = rs_sum(u, 0, 0).reshape(2, 8, cols)
+        fs[:, :, pl.ds(first, cols)] = rs_end(u).reshape(2, 8, cols)
 
     final = remote(fs.at[o], fr, x_sem.at[2], x_sem.at[3], sibling)
     final.start()
@@ -714,9 +728,9 @@
         pltpu.SemaphoreType.DMA((NU,)),
         pltpu.SemaphoreType.DMA((NU, 4)),
         pltpu.SemaphoreType.DMA((NU, 3)),
-        pltpu.SemaphoreType.DMA((NU, 18)),
+        pltpu.SemaphoreType.DMA((NU, 17)),
         pltpu.SemaphoreType.DMA((NU,)),
-        pltpu.SemaphoreType.DMA((NU, 7)),
+        pltpu.SemaphoreType.DMA((NU, 8)),
     ]
     return pl.pallas_call(
         kernel,

time: 93.7 us -> 89.3 us (0.953)
  Pallas kernels: 92 us -> 87.6 us
    pallas_call x1, Pallas kernels: 92 us -> 87.6 us  [on_device(): pl.pallas_call(kernel, out_shape=jax.ShapeDtypeStruct((8, WIDTH), BF16),...]
where the time goes in v4:
time: 89.3 us; the launch traced here: 89.2 us
  Pallas kernels  87.6 us (98%)
  local copies, waits for them, and re-layouts  1.55 us (2%)
    pallas_call x1, Pallas kernels, on_device(): pl.pallas_call(kernel, out_shape=jax.ShapeDtypeStruct((8, WIDTH), BF16),...  87.6 us

profile of v4, /device:TPU:1, one launch (start us, length us, event | category | flops | bytes accessed | tf_op | source)
XLA Modules:
  0.0 89.2 jit_solution(4476147776239850033)
XLA Ops:
  0.0 87.6 %shard_map.154 = bf16[8,7168]{1,0:T(8,128)(2,1)} custom-call(f32[3,1,56]{2,1,0:T(1,128)} %bitcast.6, f32[3,1,56]{2,1,0:T(1,128)} %bitcast.7, f32[3,1,56]{2,1,0:T(1,128)} %refs_2_.1, bf16[8,7168]{1,0:T(8,128)(2,1)} %refs_3_.1, s32[8,8]{1,0:T(8,128)} %refs_4_.1, bf16[8,8]{1,0:T(8,128)(2,1)} %refs_5_.1, bf16[3,2,16,128]{3,2,1,0:T(8,128)(2,1)} %refs_6_.1, ...), custom_call_target="tpu_custom_call" | custom-call | flops 22000001024 | bytes 25000000 | tf_op jit(solution)/shard_map/pallas_call | solution.py:735
  87.6 1.6 %copy.18 = bf16[8,7168]{1,0:T(8,128)(2,1)} copy(bf16[8,7168]{1,0:T(8,128)(2,1)} %shard_map.154) | data formatting | bytes 229376

commit v5 on v4

--- a/solution.py
+++ b/solution.py
@@ -334,11 +334,12 @@
             at_a = part(order, 2, q, r, GU)
             acc[at_a] = acc[at_a] + got[i * 64 : (i + 1) * 64].reshape(SIDE, ROWS, GU)
 
-    def from_sibling(u, rows):
+    def from_sibling(u, rows, work=True):
         n = SIDE if rows is HERE else len(rows)
         ref = blocks_of(O[u], 2, n, UNITS[u][2])
         remote(ref, ref, as_s.at[u], as_r.at[u, HAND_GROUPS.index(rows)], sibling).wait_recv()
-        gate_up(u, O[u], other0, rows)
+        if work:
+            gate_up(u, O[u], other0, rows)
 
     def shared(u, src, first0):
         _, first, cols = UNITS[u]
@@ -422,19 +423,19 @@
     for u in ALL:
         cube_a(u, -1)
     merge_down(2, 2)
-    for u in ALL:
-        gate_up(u, G[u], mine0, NEAR_A)
+    merge_down(4, 3)
     for u in ALL:
         cube_a(u, 1)
     for u in ALL:
-        from_sibling(u, NEAR_A)
-    for u in ALL:
         cube_a(u, 2)
     for u in ALL:
-        gate_up(u, G[u], mine0, NEAR_B)
-    merge_down(4, 3)
-    for u in ALL:
-        from_sibling(u, NEAR_B)
+        gate_up(u, G[u], mine0, ((None, -1),))
+        gate_up(u, G[u], mine0, ((None, 1),))
+    for u in ALL:
+        from_sibling(u, NEAR_A, False)
+        from_sibling(u, NEAR_B, False)
+        gate_up(u, O[u], other0, ((None, -1),))
+        gate_up(u, O[u], other0, ((None, 1),))
     wait_all(sgu, m_sem.at[1])
     for u in ALL:
         cube_b(u, 0)
@@ -494,6 +495,14 @@
         ns = pl.ds(pl.multiple_of(mine0 + first, LANES), cols)
         mine = dot(rows_of(u, q), dcat[:, ns]).astype(BF16)
         G[u][part(order, 2, q, None, cols)] = mine.reshape(SIDE, SIDE, ROWS, cols)
+
+    def down_near(u, first0, dst):
+        order, first, cols = UNITS[u]
+        ns = pl.ds(pl.multiple_of(first0 + first, LANES), cols)
+        lhs = jnp.concatenate([rows_of(u, 1), rows_of(u, -1)], axis=0)
+        got = dot(lhs, dcat[:, ns]).astype(BF16)
+        for i, q in enumerate((1, -1)):
+            dst[u][part(order, 2, q, None, cols)] = got[i * 256 : (i + 1) * 256].reshape(SIDE, SIDE, ROWS, cols)
 
     def take_in(u, i):
         order, _, cols = UNITS[u]
@@ -588,17 +597,16 @@
     for u in ALL:
         give(u, -1, 2).start()
         give(u, 0, 2).start()
-    for q in (1, -1):
-        for u in ALL:
-            down_other(u, q)
-            give(u, 2, q).start()
-            give(u, 1, q).start()
+    for u in ALL:
+        down_near(u, other0, O)
+        for r in (2, 1):
+            for q in (1, -1):
+                give(u, r, q).start()
     for u in ALL:
         take_in(u, 2)
         rs_far(u, 2, -1)
     for u in ALL:
-        down_mine(u, 1)
-        down_mine(u, -1)
+        down_near(u, mine0, G)
         take_in(u, 3)
         rs_near(u, 2, 2, 1)
         rs_near(u, 2, 2, -1)

time: 89.3 us -> 88.9 us (level)
  no operation moved by 1% of the time
where the time goes in v5:
time: 88.9 us; the launch traced here: 88.8 us
  Pallas kernels  87.2 us (98%)
  local copies, waits for them, and re-layouts  1.55 us (2%)
    pallas_call x1, Pallas kernels, on_device(): pl.pallas_call(kernel, out_shape=jax.ShapeDtypeStruct((8, WIDTH), BF16),...  87.2 us

profile of v5, /device:TPU:1, one launch (start us, length us, event | category | flops | bytes accessed | tf_op | source)
XLA Modules:
  0.0 88.8 jit_solution(4837700039947115959)
XLA Ops:
  0.0 87.2 %shard_map.154 = bf16[8,7168]{1,0:T(8,128)(2,1)} custom-call(f32[3,1,56]{2,1,0:T(1,128)} %bitcast.6, f32[3,1,56]{2,1,0:T(1,128)} %bitcast.7, f32[3,1,56]{2,1,0:T(1,128)} %refs_2_.1, bf16[8,7168]{1,0:T(8,128)(2,1)} %refs_3_.1, s32[8,8]{1,0:T(8,128)} %refs_4_.1, bf16[8,8]{1,0:T(8,128)(2,1)} %refs_5_.1, bf16[3,2,16,128]{3,2,1,0:T(8,128)(2,1)} %refs_6_.1, ...), custom_call_target="tpu_custom_call" | custom-call | flops 22000001024 | bytes 25000000 | tf_op jit(solution)/shard_map/pallas_call | solution.py:743
  87.2 1.6 %copy.18 = bf16[8,7168]{1,0:T(8,128)(2,1)} copy(bf16[8,7168]{1,0:T(8,128)(2,1)} %shard_map.154) | data formatting | bytes 229376
